TPU v7x, 512 devices: a whole 4x8x8 slice. The times are simulated.
512 devices in a mesh: dp: 128 (over z, y, core), tensor: 4 (over x).
Axes of the slice: x: 4, y: 8, z: 8, core: 2. Of those that a mesh axis runs over, the one named last changes fastest.
Arguments:
- master: float32 [2, 8192, 2048], P(None, 'dp', 'tensor'), may hold values from -0.0625 to 0.0625
- momentum: float32 [2, 8192, 2048], P(None, 'dp', 'tensor'), may hold values from -6 to 6
- gradient: float32 [2, 8192, 2048], P(None, 'dp', 'tensor'), may hold values from -60 to 60
- bucket_table: int32 [4, 8], P('tensor'), may hold values from 0 to 3, as said below
- tokens: bfloat16 [32768, 8192], P('dp', 'tensor'), may hold values from -6 to 6
- norm_gain: float32 [8192], replicated, may hold values from 0.1 to 1.9
Outputs:
- new_master: float32 [2, 8192, 2048], P(None, 'dp', 'tensor')
- new_momentum: float32 [2, 8192, 2048], P(None, 'dp', 'tensor')
- key_values: bfloat16 [32768, 2048], P('dp', 'tensor')
Inputs may be any that keep to these rules, and one draw needn't show every extreme that they name: `bucket_table`: in each row of 8 entries every value from 0 to 3 appears exactly twice.
All inputs are finite; a program needn't handle non-finite values.
Results may differ from a plain program's by a relative error of at most 0.001.
The roundings to bfloat16 on the way count: a program that leaves them out, or rounds other values in their place, can miss the bound.
Values may be sent and summed in bfloat16 or wider, within the bound.
A program may use at most 128 MiB of HBM per device.

v0:
```python
import math

import jax
import jax.numpy as jnp
from jax import lax
from jax.sharding import Mesh
from jax.sharding import PartitionSpec as P

D = 8192
HD = 128
NS_ITERS = 3
DP = ("dp_0", "dp_1", "dp_2")


beta_momentum = 0.95
learn_rate = 0.05
first_coeff = 3.4445
cube_coeff = -4.775
fifth_coeff = 2.0315
frob_epsilon = 1e-07
rms_epsilon = 1e-05


def rows_for(lines, count):
    spare = -len(lines) % count
    return jnp.pad(lines, [(0, spare)] + [(0, 0)] * (lines.ndim - 1))


def sent_to_all(shard, axis):
    copies = jnp.broadcast_to(shard, (lax.axis_size(axis), *shard.shape))
    return lax.all_to_all(copies, axis, split_axis=0, concat_axis=0, tiled=True)


def joined_along(pieces, dim):
    pieces = jnp.moveaxis(pieces, 0, dim)
    shape = pieces.shape
    return pieces.reshape(*shape[:dim], shape[dim] * shape[dim + 1], *shape[dim + 2 :])


def gathered_by_axis(shard, axes, dim):
    far, near = axes
    pieces = sent_to_all(sent_to_all(shard, far), near)
    return joined_along(pieces.swapaxes(0, 1).reshape(-1, *shard.shape), dim)


def in_blocks(shard, dim, count):
    shape = shard.shape
    pieces = shard.reshape(*shape[:dim], count, shape[dim] // count, *shape[dim + 1 :])
    return jnp.moveaxis(pieces, dim, 0)


def summed_on_arrival(shard, axis, dim):
    count = lax.axis_size(axis)
    pieces = lax.all_to_all(in_blocks(shard, dim, count), axis, 0, 0, tiled=True)
    return jnp.sum(pieces, axis=0)


def sum_by_axis(shard, axes, dim):
    far, near = axes
    pieces = in_blocks(shard, dim, lax.axis_size(far))
    nearer = summed_on_arrival(pieces, near, dim + 1)
    arrived = lax.all_to_all(nearer, far, split_axis=0, concat_axis=0, tiled=True)
    return arrived.sum(axis=0)


def sum_by_parts(shard, axes):
    lines = shard.reshape(-1, shard.shape[-1])
    padded = rows_for(lines, lax.axis_size(axes[0]) * lax.axis_size(axes[1]))
    whole = gathered_by_axis(sum_by_axis(padded, axes, 0), axes, 0)
    return lax.slice_in_dim(whole, 0, len(lines)).reshape(shard.shape)


def to_heads(block, head_size):
    layers = block.shape[0]
    height = block.shape[1]
    slots = block.shape[2] // head_size
    shaped = block.reshape(layers, height, slots, head_size).transpose(0, 2, 1, 3)
    return shaped.reshape(layers * slots, height, head_size)


def from_heads(heads, layers, head_size):
    count = heads.shape[0]
    height = heads.shape[1]
    slots = count // layers
    shaped = heads.reshape(layers, slots, height, head_size).transpose(0, 2, 1, 3)
    return shaped.reshape(layers, height, slots * head_size)


def stack_pairs(heads, order_ids):
    count = heads.shape[0]
    height = heads.shape[1]
    head_size = heads.shape[2]
    picked = jnp.take(heads, order_ids, axis=0)
    picked = picked.reshape(count // 2, 2, height, head_size).transpose(0, 2, 1, 3)
    return picked.reshape(count // 2, height, 2 * head_size)


def unstack_pairs(stacked, order_ids, head_size):
    pairs = stacked.shape[0]
    height = stacked.shape[1]
    split = (
        stacked.reshape(pairs, height, 2, head_size)
        .transpose(0, 2, 1, 3)
        .reshape(2 * pairs, height, head_size)
    )
    inverse = jnp.argsort(order_ids)
    return jnp.take(split, inverse, axis=0)


def local_gram(stacked):
    return jnp.einsum("brk,brj->bkj", stacked, stacked, precision=lax.Precision.HIGHEST)


def polynomial(gram_mat):
    square = jnp.einsum("bkj,bjl->bkl", gram_mat, gram_mat, precision=lax.Precision.HIGHEST)
    return cube_coeff * gram_mat + fifth_coeff * square


def per_device(master, momentum, gradient, bucket_table, tokens, norm_gain):
    new_momentum = beta_momentum * momentum + gradient
    update = gradient + beta_momentum * new_momentum
    layers = master.shape[0]
    heads = to_heads(update, HD)
    count = heads.shape[0]
    sort_keys = bucket_table[0] * count + jnp.arange(count, dtype=jnp.int32)
    order_ids = jnp.argsort(sort_keys)
    stacked = stack_pairs(heads, order_ids)
    width = stacked.shape[2]
    total = sum_by_parts(local_gram(stacked), (("dp_0", "dp_1"), "dp_2"))
    trace_sum = jnp.trace(total, axis1=1, axis2=2)
    scale = 1.0 / (jnp.sqrt(trace_sum) + frob_epsilon)
    gram_mat = total * (scale * scale)[:, None, None]
    identity = jnp.eye(width, dtype=jnp.float32)[None, :, :]
    product = jnp.broadcast_to(identity, gram_mat.shape)
    for iteration in range(NS_ITERS):
        factor = first_coeff * identity + polynomial(gram_mat)
        product = jnp.einsum("bkj,bjl->bkl", product, factor, precision=lax.Precision.HIGHEST)
        if iteration + 1 < NS_ITERS:
            gram_mat = jnp.einsum(
                "bkj,bjl,blm->bkm", factor, gram_mat, factor, precision=lax.Precision.HIGHEST
            )
    current = jnp.einsum(
        "brk,bkj->brj", stacked * scale[:, None, None], product, precision=lax.Precision.HIGHEST
    )
    ortho = from_heads(unstack_pairs(current, order_ids, HD), layers, HD)
    step_scale = learn_rate * math.sqrt(max(1.0, D / (2.0 * HD)))
    new_master = master - step_scale * ortho
    whole = lax.all_gather(tokens, "tensor", axis=1, tiled=True)
    whole_f = whole.astype(jnp.float32)
    sums = jnp.sum(whole_f * whole_f, axis=1)
    normed = (whole_f * lax.rsqrt(sums / D + rms_epsilon)[:, None] * norm_gain[None, :]).astype(
        jnp.bfloat16
    )
    first_weights = new_master[0].astype(jnp.bfloat16)
    projected = jnp.dot(
        normed,
        lax.all_gather(first_weights, DP, axis=0, tiled=True),
        preferred_element_type=jnp.float32,
    )
    return (new_master, new_momentum, projected.astype(jnp.bfloat16))


def solution(mesh):
    torus = Mesh(
        mesh.devices.reshape(8, 8, 2, mesh.shape["tensor"]), ("dp_0", "dp_1", "dp_2", "tensor")
    )
    return jax.shard_map(
        per_device,
        mesh=torus,
        in_specs=(
            P(None, DP, "tensor"),
            P(None, DP, "tensor"),
            P(None, DP, "tensor"),
            P("tensor", None),
            P(DP, "tensor"),
            P(),
        ),
        out_specs=(P(None, DP, "tensor"), P(None, DP, "tensor"), P(DP, "tensor")),
        check_vma=False,
    )
```

profile of v0, /device:TPU:1, one launch (start us, length us, event | category | flops | bytes accessed | tf_op | source)
XLA Modules:
  0.0 200.4 jit_solution(9422798814984269470)
XLA Ops:
  7.8 1.0 sort.31
  8.8 1.8 multiply_add_fusion
  11.8 1.0 fusion.35
  12.9 11.1 %all_to_all.20 = f32[2,64,8,256]{3,2,1,0:T(8,128)S(1)} all-to-all(f32[2,64,8,256]{3,2,1,0:T(8,128)S(1)} %bitcast.49), channel_id=1, replica_groups=mesh['dp_0'=8,'dp_1'=8,'dp_2'=2,'tensor'=4] {'dp_2'}, dimensions={0} | all-to-all | bytes 2097152 | tf_op jit(solution)/shard_map/all_to_all | solution.py:54
  24.0 0.9 reduce_sum.44
  24.9 10.9 %all-to-all-start.1 = ((f32[64,8,256]{2,1,0:T(8,128)}), f32[64,8,256]{2,1,0:T(8,128)S(1)}, u32[]{:S(2)}, u32[]{:S(2)}) async-start(f32[64,8,256]{2,1,0:T(8,128)} %reduce_sum.44), calls=%async_computation.1 | async-start | bytes 1048576 | tf_op jit(solution)/shard_map/all_to_all | solution.py:62
  36.5 16.9 %all-to-all-done.1 = f32[64,8,256]{2,1,0:T(8,128)S(1)} async-done(((f32[64,8,256]{2,1,0:T(8,128)}), f32[64,8,256]{2,1,0:T(8,128)S(1)}, u32[]{:S(2)}, u32[]{:S(2)}) %all-to-all-start.1) | async-done | bytes 524320 | tf_op jit(solution)/shard_map/all_to_all | solution.py:62
  54.3 6.6 %all-to-all-start.2 = ((f32[64,8,256]{2,1,0:T(8,128)}), f32[64,8,256]{2,1,0:T(8,128)S(1)}, u32[]{:S(2)}, u32[]{:S(2)}) async-start(f32[64,8,256]{2,1,0:T(8,128)} %broadcast_in_dim.38), calls=%async_computation.2 | async-start | bytes 1048576 | tf_op jit(solution)/shard_map/all_to_all | solution.py:31
  61.0 1.0 sort.32
  62.1 15.3 %all-to-all-done.2 = f32[64,8,256]{2,1,0:T(8,128)S(1)} async-done(((f32[64,8,256]{2,1,0:T(8,128)}), f32[64,8,256]{2,1,0:T(8,128)S(1)}, u32[]{:S(2)}, u32[]{:S(2)}) %all-to-all-start.2) | async-done | bytes 524320 | tf_op jit(solution)/shard_map/all_to_all | solution.py:31
  77.4 8.4 %all_to_all.21 = f32[2,64,8,256]{3,2,1,0:T(8,128)S(1)} all-to-all(f32[2,64,8,256]{3,2,1,0:T(8,128)S(1)} %broadcast_in_dim.39), channel_id=1, replica_groups=mesh['dp_0'=8,'dp_1'=8,'dp_2'=2,'tensor'=4] {'dp_2'}, dimensions={0} | all-to-all | bytes 2097152 | tf_op jit(solution)/shard_map/all_to_all | solution.py:31
  86.8 1.5 fusion.11
  88.2 1.0 fusion.25
  89.3 1.3 fusion.21
  90.6 1.2 fusion.36
  91.8 1.3 fusion.12
  93.1 1.2 fusion.38
  94.3 1.1 fusion.39
  95.4 1.1 fusion.37
  96.6 1.3 fusion.13
  97.9 1.4 fusion.40
  101.9 3.1 %fusion = f32[256]{0:T(256)S(1)} fusion(bf16[256,8192]{1,0:T(8,128)(2,1)} %all-gather.4.cloned.1.call-done), kind=kLoop, calls=%fused_computation.4 | loop fusion | flops 6291200 | bytes 4195328 | tf_op jit(solution)/shard_map/reduce_sum | solution.py:150
  105.0 80.8 %all-gather.6.cloned.1.call-done = bf16[1,8192,512]{2,1,0:T(8,128)(2,1)} async-done(((bf16[1,64,512]{2,1,0:T(8,128)(2,1)}), bf16[1,8192,512]{2,1,0:T(8,128)(2,1)}) %all-gather.6.cloned.1.call-update) | async-done | bytes 8388624 | tf_op jit(solution)/shard_map/all_gather | solution.py:157
  185.8 7.7 %fusion.14 = bf16[256,512]{1,0:T(8,128)(2,1)} fusion(bf16[1,8192,512]{2,1,0:T(8,128)(2,1)} %all-gather.6.cloned.1.call-done, bf16[256,8192]{1,0:T(8,128)(2,1)} %all-gather.4.cloned.1.call-done, f32[8192]{0:T(1024)S(1)} %copy-done.2, f32[256]{0:T(256)S(1)} %add_rsqrt_fusion), kind=kOutput, calls=%fused_computation.20 | convolution fusion | flops 2156003328 | bytes 12878848 | tf_op jit(solution)/shard_map/dot_general | solution.py:155
  (49 shorter events, 7.2 us)
Async XLA Ops:
  24.9 28.5 %all-to-all-start.1 = ((f32[64,8,256]{2,1,0:T(8,128)}), f32[64,8,256]{2,1,0:T(8,128)S(1)}, u32[]{:S(2)}, u32[]{:S(2)}) async-start(f32[64,8,256]{2,1,0:T(8,128)} %reduce_sum.44), calls=%async_computation.1 | async-start | bytes 1048576 | tf_op jit(solution)/shard_map/all_to_all | solution.py:62
  35.8 66.1 %all-gather.4.cloned.1.call-start = ((), (), s32[]{:S(2)}) async-start(), calls=%async_computation.4 | async-start | bytes 5242880 | tf_op jit(solution)/shard_map/all_gather | solution.py:148
  54.3 23.0 %all-to-all-start.2 = ((f32[64,8,256]{2,1,0:T(8,128)}), f32[64,8,256]{2,1,0:T(8,128)S(1)}, u32[]{:S(2)}, u32[]{:S(2)}) async-start(f32[64,8,256]{2,1,0:T(8,128)} %broadcast_in_dim.38), calls=%async_computation.2 | async-start | bytes 1048576 | tf_op jit(solution)/shard_map/all_to_all | solution.py:31
  60.9 124.9 %all-gather.6.cloned.1.call-start = ((), (), s32[]{:S(2)}) async-start(), calls=%async_computation.5 | async-start | bytes 8454144 | tf_op jit(solution)/shard_map/all_gather | solution.py:157
  94.3 6.8 %copy-start.1 = (f32[2,64,512]{2,1,0:T(8,128)S(1)}, f32[2,64,512]{2,1,0:T(8,128)}, u32[]{:S(2)}) copy-start(f32[2,64,512]{2,1,0:T(8,128)} %param.8) | copy-start | bytes 786436
  96.6 89.2 %copy-start.2 = (f32[8192]{0:T(1024)S(1)}, f32[8192]{0:T(1024)}, u32[]{:S(2)}) copy-start(f32[8192]{0:T(1024)} %param.13) | copy-start | bytes 98308
  101.1 92.4 %copy-start = (f32[2,64,512]{2,1,0:T(8,128)}, f32[2,64,512]{2,1,0:T(8,128)S(1)}, u32[]{:S(2)}) copy-start(f32[2,64,512]{2,1,0:T(8,128)S(1)} %sub.3) | copy-start | bytes 786436
Sparse Core Ops, SparseCore 0:
  38.7 54.2 all-gather.3
  102.0 83.7 all-gather.5
where the time goes:
time: 201 us; the launch traced here: 200 us
  waiting for transfers between devices  114 us (57%)
  matrix products  22 us (11%)
  blocking collectives  19.4 us (10%)
  starting transfers between devices  17.6 us (9%)
  between operations  14.4 us (7%)
  other arithmetic  9.5 us (5%)
  local copies, waits for them, and re-layouts  3.84 us (2%)
    all_gather x1, waiting for transfers between devices, per_device(): lax.all_gather(first_weights, DP, axis=0, tiled=True)  80.8 us
    all_to_all x1, waiting for transfers between devices, sum_by_axis(): lax.all_to_all(nearer, far, split_axis=0, concat_axis=0, tiled=True)  16.9 us
    all_to_all x1, waiting for transfers between devices, sent_to_all(): return lax.all_to_all(copies, axis, split_axis=0, concat_axis=0, tiled=True)  15.3 us
    all_to_all x1, blocking collectives, summed_on_arrival(): lax.all_to_all(in_blocks(shard, dim, count), axis, 0, 0, tiled=True)  11.1 us
    all_to_all x1, starting transfers between devices, sum_by_axis(): lax.all_to_all(nearer, far, split_axis=0, concat_axis=0, tiled=True)  10.9 us
    all_to_all x1, blocking collectives, sent_to_all(): return lax.all_to_all(copies, axis, split_axis=0, concat_axis=0, tiled=True)  8.36 us
    dot_general x1, matrix products, per_device(): jnp.dot(normed, lax.all_gather(first_weights, DP, axis=0, tiled=True), pr...  7.74 us
    all_to_all x1, starting transfers between devices, sent_to_all(): return lax.all_to_all(copies, axis, split_axis=0, concat_axis=0, tiled=True)  6.63 us
  transfers between devices with their start and end apart: 4, of which 3 were waited for; matrix products, arithmetic and copies ran while one was open for 10% of the time, Pallas kernels for 0%

commit v1 on v0

v1 whole, which is shorter than its diff:
```python
import functools
import math

import jax
import jax.numpy as jnp
from jax import lax
from jax.experimental import pallas as pl
from jax.experimental.pallas import tpu as pltpu
from jax.sharding import Mesh
from jax.sharding import PartitionSpec as P

HD = 128
NS_ITERS = 3
DP = ("dp_0", "dp_1", "dp_2")

beta_momentum = 0.95
learn_rate = 0.05
first_coeff = 3.4445
cube_coeff = -4.775
fifth_coeff = 2.0315
frob_epsilon = 1e-07
rms_epsilon = 1e-05

F32 = jnp.float32
BF16 = jnp.bfloat16
Y, Z, C, X = "dp_1", "dp_0", "dp_2", "tensor"
PACKED = 3 * HD


def near_first(n):
    offsets = [0]
    for k in range(1, n // 2):
        offsets += [k, -k]
    return [*offsets, n // 2]


def split(a):
    high = a.astype(BF16)
    return high, (a - high.astype(F32)).astype(BF16)


def dot(a, b):
    return jnp.dot(a, b, preferred_element_type=F32)


def dot3(a, b):
    return dot(a[0], b[0]) + (dot(a[0], b[1]) + dot(a[1], b[0]))


def kernel(n, d_model, table, master, momentum, gradient, tokens, gain, new_master, new_momentum,
           key_values, update, stacked, other_rows, heads, other_heads, packed, came1, part, came2,
           gram, ortho, weights, came_tokens, squares, normed, total, kv_send, kv_blocks,
           pair_send, pair_recv, gram_send, gram_recv, token_send, token_recv, first_send,
           first_recv, ring_send, ring_recv):
    half = n // 2
    rows = PACKED // n
    count = tokens.shape[0]
    blocks = tokens.shape[1] // HD
    height = master.shape[1]
    z, y, c, x = (lax.axis_index(a) for a in (Z, Y, C, X))
    axes = ((Y, Z), (Z, Y))
    place = {Y: y, Z: z}
    pending = []

    def at(axis, offset, size):
        here = {Y: y, Z: z, X: x}[axis]
        return lax.rem(here + (offset + size), size)

    def send(src, dst, sems, to):
        copy = pltpu.make_async_remote_copy(
            src_ref=src, dst_ref=dst, send_sem=sems[0], recv_sem=sems[1],
            device_id=to, device_id_type=pl.DeviceIdType.MESH,
        )
        copy.start()
        pending.append(copy)

    def arrived(ref, sems, to):
        pltpu.make_async_remote_copy(
            src_ref=ref, dst_ref=ref, send_sem=sems[0], recv_sem=sems[1],
            device_id=to, device_id_type=pl.DeviceIdType.MESH,
        ).wait_recv()

    def finish_sends():
        while pending:
            pending.pop(0).wait_send()

    partner = {C: 1 - c}

    barrier = pltpu.get_barrier_semaphore()
    greeted = [partner, {X: at(X, 1, 4)}, {X: at(X, -1, 4)}]
    for axis in (Y, Z):
        greeted += [{axis: at(axis, d, n)} for d in range(1, n)]
    for device in greeted:
        pl.semaphore_signal(barrier, inc=1, device_id=device, device_id_type=pl.DeviceIdType.MESH)

    bucket = [table[0, i] for i in range(8)]
    position = []
    for i in range(8):
        earlier = jnp.int32(0)
        for j in range(i):
            earlier += jnp.where(bucket[j] == bucket[i], 1, 0)
        position.append(2 * bucket[i] + earlier)
    held = []
    for s in range(8):
        which = jnp.int32(0)
        for i in range(8):
            which += jnp.where(position[i] == s, i, 0)
        held.append(which)

    for layer in range(2):
        for slot in range(4):
            lanes = slice(slot * HD, (slot + 1) * HD)
            g = gradient[layer, :, lanes]
            m = beta_momentum * momentum[layer, :, lanes] + g
            new_momentum[layer, :, lanes] = m
            update[layer * 4 + slot] = g + beta_momentum * m
            if layer == 0:
                heads[slot] = master[0, :, lanes]
    for s in range(8):
        stacked[s] = update[held[s]]

    pl.semaphore_wait(barrier, len(greeted))

    def pair(k):
        return pair_send.at[k], pair_recv.at[k]

    send(stacked.at[pl.ds(4 * (1 - c), 4)], other_rows, pair(0), partner)
    send(heads.at[pl.ds(2 * (1 - c), 2)], other_heads, pair(1), partner)

    right, left = {X: at(X, 1, 4)}, {X: at(X, -1, 4)}
    upper, lower = pl.ds(0, count // 2), pl.ds(count // 2, count // 2)

    def tok(k):
        return token_send.at[k], token_recv.at[k]

    send(tokens.at[upper], came_tokens.at[0, upper], tok(0), right)
    send(tokens.at[lower], came_tokens.at[2, lower], tok(1), left)
    send(tokens.at[lower], came_tokens.at[0, lower], tok(2), right)
    send(tokens.at[upper], came_tokens.at[2, upper], tok(3), left)

    arrived(other_rows, pair(0), partner)

    def chip_rows(b):
        own = jnp.concatenate([stacked[4 * c + 2 * b], stacked[4 * c + 2 * b + 1]], axis=1)
        other = jnp.concatenate([other_rows[2 * b], other_rows[2 * b + 1]], axis=1)
        return jnp.concatenate([own, other], axis=0)

    def lines(ref, net, chunk):
        return ref.at[net, pl.ds(pl.multiple_of(chunk * rows, 8), rows)]

    def gsem(stage, net, d):
        return gram_send.at[stage, net, d - 1], gram_recv.at[stage, net, d - 1]

    for net in range(2):
        s = chip_rows(net)
        g = dot3(split(s.T), split(s))
        packed[net, 0:HD] = g[:HD, :HD]
        packed[net, HD : 2 * HD] = g[:HD, HD:]
        packed[net, 2 * HD : 3 * HD] = g[HD:, HD:]
        axis = axes[net][0]
        for d in range(1, n):
            to = at(axis, d, n)
            send(lines(packed, net, to), came1.at[net, d - 1], gsem(0, net, d), {axis: to})

    def add_squares(src, fresh):
        tile = 32 if count % 32 == 0 else 16

        def body(i, _):
            r = pl.ds(pl.multiple_of(i * tile, tile), tile)
            t = jnp.zeros((tile, HD), F32) if fresh else squares[r]
            for j in range(blocks):
                v = src[r, j * HD : (j + 1) * HD].astype(F32)
                t = t + v * v
            squares[r] = t
            return 0

        lax.fori_loop(0, count // tile, body, 0)

    add_squares(tokens, True)

    for net in range(2):
        axis, other = axes[net]
        for d in range(1, n):
            arrived(came1.at[net, d - 1], gsem(0, net, d), {axis: at(axis, d, n)})
        s = packed[net, pl.ds(pl.multiple_of(place[axis] * rows, 8), rows)]
        for d in range(1, n):
            s = s + came1[net, d - 1]
        part[net] = s
        for d in range(1, n):
            send(part.at[net], came2.at[net, d - 1], gsem(1, net, d), {other: at(other, d, n)})
    for net in range(2):
        axis, other = axes[net]
        for d in range(1, n):
            arrived(came2.at[net, d - 1], gsem(1, net, d), {other: at(other, d, n)})
        s = part[net]
        for d in range(1, n):
            s = s + came2[net, d - 1]
        gram[net, pl.ds(pl.multiple_of(place[axis] * rows, 8), rows)] = s
        own = lines(gram, net, place[axis])
        for d in range(1, n):
            send(own, own, gsem(2, net, d), {axis: at(axis, d, n)})

    arrived(came_tokens.at[0, upper], tok(0), right)
    send(came_tokens.at[0, upper], came_tokens.at[1, upper], tok(4), right)
    arrived(came_tokens.at[2, lower], tok(1), left)
    send(came_tokens.at[2, lower], came_tokens.at[1, lower], tok(5), left)

    for net in range(2):
        axis = axes[net][0]
        for d in range(1, n):
            arrived(lines(gram, net, at(axis, -d, n)), gsem(2, net, d), {axis: at(axis, d, n)})

    r_id = lax.broadcasted_iota(jnp.int32, (2 * HD, 2 * HD), 0)
    c_id = lax.broadcasted_iota(jnp.int32, (2 * HD, 2 * HD), 1)
    eye = jnp.where(r_id == c_id, 1.0, 0.0).astype(F32)
    grams, scales, products = [], [], [None, None]
    for net in range(2):
        corner = gram[net, HD : 2 * HD]
        top = jnp.concatenate([gram[net, 0:HD], corner], axis=1)
        bottom = jnp.concatenate([corner.T, gram[net, 2 * HD : 3 * HD]], axis=1)
        g = jnp.concatenate([top, bottom], axis=0)
        trace = jnp.sum(jnp.sum(g * eye, axis=1, keepdims=True), axis=0, keepdims=True)
        scale = 1.0 / (jnp.sqrt(trace) + frob_epsilon)
        grams.append(g * (scale * scale))
        scales.append(scale)
    for iteration in range(NS_ITERS):
        gs = [split(g) for g in grams]
        squared = [dot3(g, g) for g in gs]
        factor = [
            first_coeff * eye + (cube_coeff * g + fifth_coeff * q) for g, q in zip(grams, squared)
        ]
        fs = [split(f) for f in factor]
        if iteration == 0:
            products = factor
        else:
            products = [dot3(split(p), f) for p, f in zip(products, fs)]
        if iteration + 1 < NS_ITERS:
            half_way = [dot3(f, g) for f, g in zip(fs, gs)]
            grams = [dot3(split(h), f) for h, f in zip(half_way, fs)]

    step = learn_rate * math.sqrt(max(1.0, d_model / (2.0 * HD)))
    for net in range(2):
        moved = dot3(split(chip_rows(net)), split(products[net] * (scales[net] * step)))
        for h in range(2):
            lanes = slice(h * HD, (h + 1) * HD)
            ortho[4 * c + 2 * net + h, c] = moved[:height, lanes]
            ortho[4 * c + 2 * net + h, 1 - c] = moved[height:, lanes]
    mine = ortho.at[pl.ds(4 * c, 4)]
    send(mine, mine, pair(2), partner)
    arrived(other_heads, pair(1), partner)
    arrived(ortho.at[pl.ds(4 * (1 - c), 4)], pair(2), partner)

    order = near_first(n)
    slot_of = {o % n: k for k, o in enumerate(order)}
    ring_axis = (Z, Y)

    def fsem(net, d):
        return first_send.at[net, d - 1], first_recv.at[net, d - 1]

    for net in range(2):
        where = jnp.where(c == 0, position[net], position[2 + net])
        block = place[ring_axis[net]]
        weights[net, block, 0, c] = (heads[2 * c + net] - ortho[where, c]).astype(BF16)
        weights[net, block, 0, 1 - c] = (other_heads[net] - ortho[where, 1 - c]).astype(BF16)
        axis = axes[net][0]
        for o in order[1:]:
            d = o % n
            send(weights.at[net, block, 0], weights.at[net, block, slot_of[-o % n]], fsem(net, d),
                 {axis: at(axis, d, n)})

    for i in range(8):
        lanes = slice((i % 4) * HD, (i % 4 + 1) * HD)
        new_master[i // 4, :, lanes] = master[i // 4, :, lanes] - ortho[position[i], c]

    def first_came(net, group):
        axis = axes[net][0]
        for k in range(max(1, group * half), (group + 1) * half):
            d = -order[k] % n
            arrived(weights.at[net, place[ring_axis[net]], k], fsem(net, d), {axis: at(axis, d, n)})

    def rsem(net, way, s, h):
        return ring_send.at[net, way, s, h], ring_recv.at[net, way, s, h]

    def sub(net, offset, h):
        return weights.at[net, at(ring_axis[net], offset, n), pl.ds(h * half, half)]

    def goes(way, s, h):
        return s + 1 < half or way == h

    seen = set()

    def need(net, way, s, h):
        if (net, way, s, h) in seen or not goes(way, s, h):
            return
        seen.add((net, way, s, h))
        sign = 1 if way == 0 else -1
        arrived(sub(net, -sign * (s + 1), h), rsem(net, way, s, h),
                {ring_axis[net]: at(ring_axis[net], sign, n)})

    def ring(s, h):
        for net in range(2):
            if s == 0:
                first_came(net, h)
            for way in range(2):
                if s > 0:
                    if not goes(way, s, h):
                        continue
                    need(net, way, s - 1, h)
                if goes(way, s, h):
                    sign = 1 if way == 0 else -1
                    moving = sub(net, -sign * s, h)
                    send(moving, moving, rsem(net, way, s, h),
                         {ring_axis[net]: at(ring_axis[net], sign, n)})

    def inverse_rms():
        mean = jnp.sum(squares[...], axis=1, keepdims=True) / d_model
        squares[...] = jnp.broadcast_to(lax.rsqrt(mean + rms_epsilon), squares.shape)

    def normalise(src, offset, k):
        tile = 32 if count % 32 == 0 else 16
        first = at(X, offset, 4) * blocks

        def body(i, _):
            r = pl.ds(pl.multiple_of(i * tile, tile), tile)
            inverse = squares[r]
            for j in range(blocks):
                v = src[r, j * HD : (j + 1) * HD].astype(F32)
                v = v * inverse * gain[pl.ds(first + j, 1), :]
                normed[first + j, c, r] = v.astype(BF16)
            return 0

        lax.fori_loop(0, count // tile, body, 0)
        made = normed.at[pl.ds(first, blocks), c]
        send(made, made, pair(3 + k), partner)

    def partner_normed(offset, k):
        first = at(X, offset, 4) * blocks
        arrived(normed.at[pl.ds(first, blocks), 1 - c], pair(3 + k), partner)

    def multiply(net, offset, fresh=False):
        block = at(ring_axis[net], offset, n)
        axis = axes[net][0]
        wide = []
        for o in order:
            across = at(axis, o, n)
            feature = block * n + across if net == 0 else across * n + block
            wide.append(normed[feature].reshape(2 * count, HD))
        product = dot(jnp.concatenate(wide, axis=1), weights[net, block].reshape(n * HD, HD))
        total[net] = product if fresh else total[net] + product

    def tokens_one():
        arrived(came_tokens.at[0, lower], tok(2), right)
        add_squares(came_tokens.at[0], False)

    def tokens_three():
        arrived(came_tokens.at[2, upper], tok(3), left)
        add_squares(came_tokens.at[2], False)

    def tokens_two():
        arrived(came_tokens.at[1, upper], tok(4), right)
        arrived(came_tokens.at[1, lower], tok(5), left)
        add_squares(came_tokens.at[1], False)
        inverse_rms()

    def own_block():
        for k, offset in enumerate((0, -1, 1, 2)):
            partner_normed(offset, k)
        for net in range(2):
            multiply(net, 0, True)

    def distance(k):
        for net in range(2):
            for h in range(2):
                for way in range(2):
                    need(net, way, k - 1, h)
            multiply(net, k)
            if k < half:
                multiply(net, -k)

    work = [
        [tokens_one],
        [tokens_three, tokens_two],
        [lambda: normalise(tokens, 0, 0), lambda: normalise(came_tokens.at[0], -1, 1)],
        [lambda: normalise(came_tokens.at[2], 1, 2), lambda: normalise(came_tokens.at[1], 2, 3)],
        [own_block],
        [functools.partial(distance, 1)],
    ]
    work += [[functools.partial(distance, k)] for k in range(2, half + 1)]
    for s in range(half):
        for h in range(2):
            ring(s, h)
            if s + 1 == half and half > 1 and h == 0:
                continue
            for task in work.pop(0):
                task()
    for tasks in work:
        for task in tasks:
            task()

    for net in range(2):
        kv_send[net] = total[net, pl.ds(pl.multiple_of((1 - c) * count, 16), count)].astype(BF16)
    send(kv_send, kv_blocks.at[pl.ds(2 * c, 2)], pair(7), partner)
    for net in range(2):
        kv_blocks[2 * c + net] = total[net, pl.ds(pl.multiple_of(c * count, 16), count)].astype(BF16)
    arrived(kv_blocks.at[pl.ds(2 * (1 - c), 2)], pair(7), partner)
    for k in range(4):
        key_values[:, k * HD : (k + 1) * HD] = kv_blocks[k]
    finish_sends()


def per_device(n, d_model, master, momentum, gradient, bucket_table, tokens, norm_gain):
    height = master.shape[1]
    count, width = tokens.shape
    blocks = width // HD
    rows = PACKED // n
    half = n // 2
    vmem = pl.BlockSpec(memory_space=pltpu.VMEM)
    dma = pltpu.SemaphoreType.DMA
    scratch = [
        pltpu.VMEM((8, height, HD), F32),
        pltpu.VMEM((8, height, HD), F32),
        pltpu.VMEM((4, height, HD), F32),
        pltpu.VMEM((4, height, HD), F32),
        pltpu.VMEM((2, height, HD), F32),
        pltpu.VMEM((2, PACKED, HD), F32),
        pltpu.VMEM((2, n - 1, rows, HD), F32),
        pltpu.VMEM((2, rows, HD), F32),
        pltpu.VMEM((2, n - 1, rows, HD), F32),
        pltpu.VMEM((2, PACKED, HD), F32),
        pltpu.VMEM((8, 2, height, HD), F32),
        pltpu.VMEM((2, n, n, 2, height, HD), BF16),
        pltpu.VMEM((3, count, width), BF16),
        pltpu.VMEM((count, HD), F32),
        pltpu.VMEM((4 * blocks, 2, count, HD), BF16),
        pltpu.VMEM((2, 2 * count, HD), F32),
        pltpu.VMEM((2, count, HD), BF16),
        pltpu.VMEM((4, count, HD), BF16),
        dma((8,)),
        dma((8,)),
        dma((3, 2, n - 1)),
        dma((3, 2, n - 1)),
        dma((6,)),
        dma((6,)),
        dma((2, n - 1)),
        dma((2, n - 1)),
        dma((2, 2, half, 2)),
        dma((2, 2, half, 2)),
    ]
    return pl.pallas_call(
        functools.partial(kernel, n, d_model),
        out_shape=(
            jax.ShapeDtypeStruct(master.shape, F32),
            jax.ShapeDtypeStruct(master.shape, F32),
            jax.ShapeDtypeStruct((count, 4 * HD), BF16),
        ),
        in_specs=[pl.BlockSpec(memory_space=pltpu.SMEM), vmem, vmem, vmem, vmem, vmem],
        out_specs=(vmem, vmem, vmem),
        scratch_shapes=scratch,
        compiler_params=pltpu.CompilerParams(
            collective_id=0, has_side_effects=True, vmem_limit_bytes=48 * 1024 * 1024
        ),
    )(bucket_table, master, momentum, gradient, tokens, norm_gain.reshape(-1, HD))


def solution(mesh):
    n = math.isqrt(mesh.shape["dp"] // 2)
    torus = Mesh(
        mesh.devices.reshape(n, n, 2, mesh.shape["tensor"]), ("dp_0", "dp_1", "dp_2", "tensor")
    )

    def whole(*args):
        return jax.shard_map(
            functools.partial(per_device, n, args[0].shape[1]),
            mesh=torus,
            in_specs=(
                P(None, DP, "tensor"),
                P(None, DP, "tensor"),
                P(None, DP, "tensor"),
                P("tensor", None),
                P(DP, "tensor"),
                P(),
            ),
            out_specs=(P(None, DP, "tensor"), P(None, DP, "tensor"), P(DP, "tensor")),
            check_vma=False,
        )(*args)

    return whole
```

time: 201 us -> 86.5 us (0.43)
  waiting for transfers between devices: 114 us -> 0 us
  Pallas kernels: 0 us -> 78 us
  matrix products: 22 us -> 0 us
  blocking collectives: 19.4 us -> 0 us
  starting transfers between devices: 17.6 us -> 0 us
  between operations: 14.4 us -> 0.65 us
  other arithmetic: 9.5 us -> 0 us
  local copies, waits for them, and re-layouts: 3.84 us -> 7.59 us
    all_gather x2 -> x0, waiting for transfers between devices: 80.8 us -> none  [the longest x1 80.8 us: per_device(): lax.all_gather(first_weights, DP, axis=0, tiled=True)]
    pallas_call x0 -> x1, Pallas kernels: none -> 78 us  [per_device(): pl.pallas_call(functools.partial(kernel, n, d_model), out_shape=(jax.Shap...]
    all_to_all x2 -> x0, waiting for transfers between devices: 32.1 us -> none  [the longest x1 16.9 us: sum_by_axis(): lax.all_to_all(nearer, far, split_axis=0, concat_axis=0, tiled=True)]
    dot_general x13 -> x0, matrix products: 22 us -> none  [the longest x1 7.74 us: per_device(): jnp.dot(normed, lax.all_gather(first_weights, DP, axis=0, tiled=True), pr...]
    all_to_all x2 -> x0, blocking collectives: 19.4 us -> none  [the longest x1 11.1 us: summed_on_arrival(): lax.all_to_all(in_blocks(shard, dim, count), axis, 0, 0, tiled=True)]
    all_to_all x2 -> x0, starting transfers between devices: 17.6 us -> none  [the longest x1 10.9 us: sum_by_axis(): lax.all_to_all(nearer, far, split_axis=0, concat_axis=0, tiled=True)]
    unnamed x6 -> x15, local copies, waits for them, and re-layouts: 0.02 us -> 7.59 us
    reduce_sum x5 -> x0, other arithmetic: 4.75 us -> none  [the longest x1 3.1 us: per_device(): sums = jnp.sum(whole_f * whole_f, axis=1)]
  transfers between devices with their start and end apart: 4 -> 0, of which waited for: 3 -> 0; matrix products, arithmetic and copies ran while one was open for 10% -> 0% of each run, Pallas kernels for 0% -> 0%
where the time goes in v1:
time: 86.5 us; the launch traced here: 86.2 us
  Pallas kernels  78 us (90%)
  local copies, waits for them, and re-layouts  7.59 us (9%)
    pallas_call x1, Pallas kernels, per_device(): pl.pallas_call(functools.partial(kernel, n, d_model), out_shape=(jax.Shap...  78 us
    unnamed x15, local copies, waits for them, and re-layouts  7.59 us

profile of v1, /device:TPU:1, one launch (start us, length us, event | category | flops | bytes accessed | tf_op | source)
XLA Modules:
  0.0 86.2 jit_solution(9187157596236954697)
XLA Ops:
  0.6 0.0 copy-start.5
  0.6 0.6 copy-done.5
  1.3 0.0 copy-start
  1.3 1.2 %copy-done = bf16[256,2048]{1,0:T(8,128)(2,1)S(1)} copy-done((bf16[256,2048]{1,0:T(8,128)(2,1)S(1)}, bf16[256,2048]{1,0:T(8,128)(2,1)}, u32[]{:S(2)}) %copy-start) | copy-done | bytes 1048600
  2.5 0.0 copy-start.1
  2.5 0.9 %copy-done.1 = f32[2,64,512]{2,1,0:T(8,128)S(1)} copy-done((f32[2,64,512]{2,1,0:T(8,128)S(1)}, f32[2,64,512]{2,1,0:T(8,128)}, u32[]{:S(2)}) %copy-start.1) | copy-done | bytes 262168
  3.5 0.0 copy-start.2
  3.5 0.9 %copy-done.2 = f32[2,64,512]{2,1,0:T(8,128)S(1)} copy-done((f32[2,64,512]{2,1,0:T(8,128)S(1)}, f32[2,64,512]{2,1,0:T(8,128)}, u32[]{:S(2)}) %copy-start.2) | copy-done | bytes 262168
  4.4 0.0 copy-start.3
  4.4 0.9 %copy-done.3 = f32[2,64,512]{2,1,0:T(8,128)S(1)} copy-done((f32[2,64,512]{2,1,0:T(8,128)S(1)}, f32[2,64,512]{2,1,0:T(8,128)}, u32[]{:S(2)}) %copy-start.3) | copy-done | bytes 262168
  5.4 0.0 copy-start.4
  5.4 0.8 copy-done.4
  6.1 78.0 %shard_map.85 = (f32[2,64,512]{2,1,0:T(8,128)S(1)}, f32[2,64,512]{2,1,0:T(8,128)S(1)}, bf16[256,512]{1,0:T(8,128)(2,1)S(1)}) custom-call(s32[1,8]{1,0:T(1,128)S(1)} %copy-done.5, f32[2,64,512]{2,1,0:T(8,128)S(1)} %copy-done.1, f32[2,64,512]{2,1,0:T(8,128)S(1)} %copy-done.2, f32[2,64,512]{2,1,0:T(8,128)S(1)} %copy-done.3, bf16[256,2048]{1,0:T(8,128)(2,1)S(1)} %copy-done, ...), custom_call_target="tpu_custom_call" | custom-call | tf_op jit(solution)/shard_map/pallas_call | solution.py:449
  84.1 0.7 copy.12
  84.8 0.7 copy.13
  85.5 0.7 copy.14
Async XLA Ops:
  0.6 0.7 copy-start.5
  1.3 1.2 %copy-start = (bf16[256,2048]{1,0:T(8,128)(2,1)S(1)}, bf16[256,2048]{1,0:T(8,128)(2,1)}, u32[]{:S(2)}) copy-start(bf16[256,2048]{1,0:T(8,128)(2,1)} %tokens.1) | copy-start | bytes 3145732
  2.5 0.9 %copy-start.1 = (f32[2,64,512]{2,1,0:T(8,128)S(1)}, f32[2,64,512]{2,1,0:T(8,128)}, u32[]{:S(2)}) copy-start(f32[2,64,512]{2,1,0:T(8,128)} %master.1) | copy-start | bytes 786436
  3.5 0.9 %copy-start.2 = (f32[2,64,512]{2,1,0:T(8,128)S(1)}, f32[2,64,512]{2,1,0:T(8,128)}, u32[]{:S(2)}) copy-start(f32[2,64,512]{2,1,0:T(8,128)} %momentum.1) | copy-start | bytes 786436
  4.4 0.9 %copy-start.3 = (f32[2,64,512]{2,1,0:T(8,128)S(1)}, f32[2,64,512]{2,1,0:T(8,128)}, u32[]{:S(2)}) copy-start(f32[2,64,512]{2,1,0:T(8,128)} %gradient.1) | copy-start | bytes 786436
  5.4 0.8 copy-start.4

commit v2 on v1

--- a/solution.py
+++ b/solution.py
@@ -24,7 +24,7 @@
 F32 = jnp.float32
 BF16 = jnp.bfloat16
 Y, Z, C, X = "dp_1", "dp_0", "dp_2", "tensor"
-PACKED = 3 * HD
+PACKED = 2 * HD + 64
 
 
 def near_first(n):
@@ -47,11 +47,12 @@
     return dot(a[0], b[0]) + (dot(a[0], b[1]) + dot(a[1], b[0]))
 
 
-def kernel(n, d_model, table, master, momentum, gradient, tokens, gain, new_master, new_momentum,
-           key_values, update, stacked, other_rows, heads, other_heads, packed, came1, part, came2,
-           gram, ortho, weights, came_tokens, squares, normed, total, kv_send, kv_blocks,
-           pair_send, pair_recv, gram_send, gram_recv, token_send, token_recv, first_send,
-           first_recv, ring_send, ring_recv):
+def kernel(n, d_model, table_in, master_in, momentum_in, gradient_in, tokens_in, gain_in, new_master,
+           new_momentum, key_values, table, master, momentum, gradient, tokens, gain, load, store, update,
+           stacked, other_rows, heads, other_heads, packed, came1, part, came2, gram, ortho, weights,
+           came_tokens, squares, normed, total, kv_send, kv_blocks, pair_send, pair_recv, gram_send,
+           gram_recv, token_send, token_recv, first_send, first_recv, begin_send, begin_recv, ring_send,
+           ring_recv):
     half = n // 2
     rows = PACKED // n
     count = tokens.shape[0]
@@ -92,6 +93,17 @@
         greeted += [{axis: at(axis, d, n)} for d in range(1, n)]
     for device in greeted:
         pl.semaphore_signal(barrier, inc=1, device_id=device, device_id_type=pl.DeviceIdType.MESH)
+
+    loads = [
+        pltpu.make_async_copy(src, dst, load.at[k])
+        for k, (src, dst) in enumerate((
+            (table_in, table), (gradient_in, gradient), (momentum_in, momentum),
+            (master_in, master), (tokens_in, tokens), (gain_in, gain),
+        ))
+    ]
+    for copy in loads:
+        copy.start()
+    loads[0].wait()
 
     bucket = [table[0, i] for i in range(8)]
     position = []
@@ -107,17 +119,21 @@
             which += jnp.where(position[i] == s, i, 0)
         held.append(which)
 
+    for copy in loads[1:4]:
+        copy.wait()
     for layer in range(2):
         for slot in range(4):
             lanes = slice(slot * HD, (slot + 1) * HD)
             g = gradient[layer, :, lanes]
             m = beta_momentum * momentum[layer, :, lanes] + g
-            new_momentum[layer, :, lanes] = m
+            momentum[layer, :, lanes] = m
             update[layer * 4 + slot] = g + beta_momentum * m
             if layer == 0:
                 heads[slot] = master[0, :, lanes]
     for s in range(8):
         stacked[s] = update[held[s]]
+    stores = [pltpu.make_async_copy(momentum, new_momentum, store.at[0])]
+    stores[0].start()
 
     pl.semaphore_wait(barrier, len(greeted))
 
@@ -129,6 +145,9 @@
 
     right, left = {X: at(X, 1, 4)}, {X: at(X, -1, 4)}
     upper, lower = pl.ds(0, count // 2), pl.ds(count // 2, count // 2)
+
+    for copy in loads[4:]:
+        copy.wait()
 
     def tok(k):
         return token_send.at[k], token_recv.at[k]
@@ -148,17 +167,23 @@
     def lines(ref, net, chunk):
         return ref.at[net, pl.ds(pl.multiple_of(chunk * rows, 8), rows)]
 
+    far_first = [o % n for o in reversed(near_first(n)[1:])]
+
     def gsem(stage, net, d):
         return gram_send.at[stage, net, d - 1], gram_recv.at[stage, net, d - 1]
 
+    r_id = lax.broadcasted_iota(jnp.int32, (HD, HD), 0)
+    c_id = lax.broadcasted_iota(jnp.int32, (HD, HD), 1)
     for net in range(2):
         s = chip_rows(net)
         g = dot3(split(s.T), split(s))
-        packed[net, 0:HD] = g[:HD, :HD]
+        second = g[HD:, HD:]
+        packed[net, 0:HD] = jnp.where(r_id <= c_id, g[:HD, :HD], second)
         packed[net, HD : 2 * HD] = g[:HD, HD:]
-        packed[net, 2 * HD : 3 * HD] = g[HD:, HD:]
+        diagonal = jnp.sum(jnp.where(r_id == c_id, second, 0.0), axis=0, keepdims=True)
+        packed[net, 2 * HD :] = jnp.broadcast_to(diagonal, (PACKED - 2 * HD, HD))
         axis = axes[net][0]
-        for d in range(1, n):
+        for d in far_first:
             to = at(axis, d, n)
             send(lines(packed, net, to), came1.at[net, d - 1], gsem(0, net, d), {axis: to})
 
@@ -186,7 +211,7 @@
         for d in range(1, n):
             s = s + came1[net, d - 1]
         part[net] = s
-        for d in range(1, n):
+        for d in far_first:
             send(part.at[net], came2.at[net, d - 1], gsem(1, net, d), {other: at(other, d, n)})
     for net in range(2):
         axis, other = axes[net]
@@ -197,7 +222,7 @@
             s = s + came2[net, d - 1]
         gram[net, pl.ds(pl.multiple_of(place[axis] * rows, 8), rows)] = s
         own = lines(gram, net, place[axis])
-        for d in range(1, n):
+        for d in far_first:
             send(own, own, gsem(2, net, d), {axis: at(axis, d, n)})
 
     arrived(came_tokens.at[0, upper], tok(0), right)
@@ -210,14 +235,18 @@
         for d in range(1, n):
             arrived(lines(gram, net, at(axis, -d, n)), gsem(2, net, d), {axis: at(axis, d, n)})
 
-    r_id = lax.broadcasted_iota(jnp.int32, (2 * HD, 2 * HD), 0)
-    c_id = lax.broadcasted_iota(jnp.int32, (2 * HD, 2 * HD), 1)
-    eye = jnp.where(r_id == c_id, 1.0, 0.0).astype(F32)
+    eye = jnp.where(
+        lax.broadcasted_iota(jnp.int32, (2 * HD, 2 * HD), 0)
+        == lax.broadcasted_iota(jnp.int32, (2 * HD, 2 * HD), 1), 1.0, 0.0
+    ).astype(F32)
     grams, scales, products = [], [], [None, None]
     for net in range(2):
-        corner = gram[net, HD : 2 * HD]
-        top = jnp.concatenate([gram[net, 0:HD], corner], axis=1)
-        bottom = jnp.concatenate([corner.T, gram[net, 2 * HD : 3 * HD]], axis=1)
+        both, corner = gram[net, 0:HD], gram[net, HD : 2 * HD]
+        turned = both.T
+        one = jnp.where(r_id <= c_id, both, turned)
+        two = jnp.where(r_id > c_id, both, jnp.where(r_id < c_id, turned, gram[net, 2 * HD : 2 * HD + 1]))
+        top = jnp.concatenate([one, corner], axis=1)
+        bottom = jnp.concatenate([corner.T, two], axis=1)
         g = jnp.concatenate([top, bottom], axis=0)
         trace = jnp.sum(jnp.sum(g * eye, axis=1, keepdims=True), axis=0, keepdims=True)
         scale = 1.0 / (jnp.sqrt(trace) + frob_epsilon)
@@ -254,38 +283,43 @@
     slot_of = {o % n: k for k, o in enumerate(order)}
     ring_axis = (Z, Y)
 
-    def fsem(net, d):
-        return first_send.at[net, d - 1], first_recv.at[net, d - 1]
-
-    for net in range(2):
-        where = jnp.where(c == 0, position[net], position[2 + net])
-        block = place[ring_axis[net]]
-        weights[net, block, 0, c] = (heads[2 * c + net] - ortho[where, c]).astype(BF16)
-        weights[net, block, 0, 1 - c] = (other_heads[net] - ortho[where, 1 - c]).astype(BF16)
-        axis = axes[net][0]
-        for o in order[1:]:
-            d = o % n
-            send(weights.at[net, block, 0], weights.at[net, block, slot_of[-o % n]], fsem(net, d),
-                 {axis: at(axis, d, n)})
-
-    for i in range(8):
-        lanes = slice((i % 4) * HD, (i % 4 + 1) * HD)
-        new_master[i // 4, :, lanes] = master[i // 4, :, lanes] - ortho[position[i], c]
-
-    def first_came(net, group):
-        axis = axes[net][0]
-        for k in range(max(1, group * half), (group + 1) * half):
-            d = -order[k] % n
-            arrived(weights.at[net, place[ring_axis[net]], k], fsem(net, d), {axis: at(axis, d, n)})
-
     def rsem(net, way, s, h):
         return ring_send.at[net, way, s, h], ring_recv.at[net, way, s, h]
 
+    def bsem(net, way, k):
+        return begin_send.at[net, way, k], begin_recv.at[net, way, k]
+
+    def fsem(net, k):
+        return first_send.at[net, k], first_recv.at[net, k]
+
     def sub(net, offset, h):
         return weights.at[net, at(ring_axis[net], offset, n), pl.ds(h * half, half)]
 
+    def piece(net, offset, k):
+        return weights.at[net, at(ring_axis[net], offset, n), k]
+
     def goes(way, s, h):
         return s + 1 < half or way == h
+
+    def pass_on(net, j):
+        axis = axes[net][0]
+        if j + 1 < half:
+            for sign in (1, -1):
+                k = slot_of[sign * (j + 1) % n]
+                send(piece(net, 0, slot_of[sign * j % n]), piece(net, 0, k), fsem(net, k),
+                     {axis: at(axis, -sign, n)})
+        elif j + 1 == half:
+            k = slot_of[half]
+            source = jnp.where(c == 0, slot_of[j % n], slot_of[-j % n])
+            send(piece(net, 0, source), piece(net, 0, k), fsem(net, k), {axis: at(axis, 2 * c - 1, n)})
+
+    def begin(net, j):
+        for k in sorted({slot_of[j % n], slot_of[-j % n]}):
+            for way, sign in enumerate((1, -1)):
+                if goes(way, 0, k // half):
+                    moving = piece(net, 0, k)
+                    send(moving, moving, bsem(net, way, k),
+                         {ring_axis[net]: at(ring_axis[net], sign, n)})
 
     seen = set()
 
@@ -294,23 +328,44 @@
             return
         seen.add((net, way, s, h))
         sign = 1 if way == 0 else -1
-        arrived(sub(net, -sign * (s + 1), h), rsem(net, way, s, h),
-                {ring_axis[net]: at(ring_axis[net], sign, n)})
+        to = {ring_axis[net]: at(ring_axis[net], sign, n)}
+        if s == 0:
+            for k in range(h * half, (h + 1) * half):
+                arrived(piece(net, -sign, k), bsem(net, way, k), to)
+        else:
+            arrived(sub(net, -sign * (s + 1), h), rsem(net, way, s, h), to)
 
     def ring(s, h):
         for net in range(2):
-            if s == 0:
-                first_came(net, h)
-            for way in range(2):
-                if s > 0:
-                    if not goes(way, s, h):
-                        continue
+            for way, sign in enumerate((1, -1)):
+                if goes(way, s, h):
                     need(net, way, s - 1, h)
-                if goes(way, s, h):
-                    sign = 1 if way == 0 else -1
                     moving = sub(net, -sign * s, h)
                     send(moving, moving, rsem(net, way, s, h),
                          {ring_axis[net]: at(ring_axis[net], sign, n)})
+
+    for net in range(2):
+        where = jnp.where(c == 0, position[net], position[2 + net])
+        block = place[ring_axis[net]]
+        weights[net, block, 0, c] = (heads[2 * c + net] - ortho[where, c]).astype(BF16)
+        weights[net, block, 0, 1 - c] = (other_heads[net] - ortho[where, 1 - c]).astype(BF16)
+        pass_on(net, 0)
+        begin(net, 0)
+    for j in range(1, half + 1):
+        for net in range(2):
+            axis = axes[net][0]
+            for k in sorted({slot_of[j % n], slot_of[-j % n]}):
+                arrived(piece(net, 0, k), fsem(net, k), {axis: at(axis, 1, n)})
+            pass_on(net, j)
+            begin(net, j)
+        if j + 1 == half:
+            ring(1, 0)
+
+    for i in range(8):
+        lanes = slice((i % 4) * HD, (i % 4 + 1) * HD)
+        master[i // 4, :, lanes] = master[i // 4, :, lanes] - ortho[position[i], c]
+    stores.append(pltpu.make_async_copy(master, new_master, store.at[1]))
+    stores[1].start()
 
     def inverse_rms():
         mean = jnp.sum(squares[...], axis=1, keepdims=True) / d_model
@@ -382,17 +437,14 @@
         [tokens_three, tokens_two],
         [lambda: normalise(tokens, 0, 0), lambda: normalise(came_tokens.at[0], -1, 1)],
         [lambda: normalise(came_tokens.at[2], 1, 2), lambda: normalise(came_tokens.at[1], 2, 3)],
-        [own_block],
-        [functools.partial(distance, 1)],
+        [own_block, functools.partial(distance, 1)],
     ]
     work += [[functools.partial(distance, k)] for k in range(2, half + 1)]
-    for s in range(half):
-        for h in range(2):
-            ring(s, h)
-            if s + 1 == half and half > 1 and h == 0:
-                continue
-            for task in work.pop(0):
-                task()
+    steps = [(s, h) for s in range(1, half) for h in range(2) if (s, h) != (1, 0)]
+    for s, h in steps:
+        for task in work.pop(0):
+            task()
+        ring(s, h)
     for tasks in work:
         for task in tasks:
             task()
@@ -402,10 +454,31 @@
     send(kv_send, kv_blocks.at[pl.ds(2 * c, 2)], pair(7), partner)
     for net in range(2):
         kv_blocks[2 * c + net] = total[net, pl.ds(pl.multiple_of(c * count, 16), count)].astype(BF16)
+
+    def store_columns(core, k):
+        for net in range(2):
+            block = 2 * core + net
+            lanes = pl.ds(pl.multiple_of(block * HD, HD), HD)
+            stores.append(
+                pltpu.make_async_copy(kv_blocks.at[block], key_values.at[:, lanes], store.at[k + net])
+            )
+            stores[-1].start()
+
+    store_columns(c, 2)
+    finish_sends()
     arrived(kv_blocks.at[pl.ds(2 * (1 - c), 2)], pair(7), partner)
-    for k in range(4):
-        key_values[:, k * HD : (k + 1) * HD] = kv_blocks[k]
-    finish_sends()
+    store_columns(1 - c, 4)
+    for copy in stores:
+        copy.wait()
+
+
+def hand_over(*refs):
+    given, taken, done = refs[:3], refs[3:6], refs[6]
+    copies = [pltpu.make_async_copy(a, b, done.at[k]) for k, (a, b) in enumerate(zip(given, taken))]
+    for copy in copies:
+        copy.start()
+    for copy in copies:
+        copy.wait()
 
 
 def per_device(n, d_model, master, momentum, gradient, bucket_table, tokens, norm_gain):
@@ -414,9 +487,15 @@
     blocks = width // HD
     rows = PACKED // n
     half = n // 2
-    vmem = pl.BlockSpec(memory_space=pltpu.VMEM)
+    anywhere = pl.BlockSpec(memory_space=pl.ANY)
     dma = pltpu.SemaphoreType.DMA
     scratch = [
+        pltpu.SMEM(bucket_table.shape, jnp.int32),
+        *[pltpu.VMEM(master.shape, F32) for _ in range(3)],
+        pltpu.VMEM(tokens.shape, BF16),
+        pltpu.VMEM((4 * blocks, HD), F32),
+        dma((6,)),
+        dma((6,)),
         pltpu.VMEM((8, height, HD), F32),
         pltpu.VMEM((8, height, HD), F32),
         pltpu.VMEM((4, height, HD), F32),
@@ -441,25 +520,35 @@
         dma((3, 2, n - 1)),
         dma((6,)),
         dma((6,)),
-        dma((2, n - 1)),
-        dma((2, n - 1)),
+        dma((2, n)),
+        dma((2, n)),
+        dma((2, 2, n)),
+        dma((2, 2, n)),
         dma((2, 2, half, 2)),
         dma((2, 2, half, 2)),
     ]
-    return pl.pallas_call(
+    outs = (
+        jax.ShapeDtypeStruct(master.shape, F32),
+        jax.ShapeDtypeStruct(master.shape, F32),
+        jax.ShapeDtypeStruct((count, 4 * HD), BF16),
+    )
+    made = pl.pallas_call(
         functools.partial(kernel, n, d_model),
-        out_shape=(
-            jax.ShapeDtypeStruct(master.shape, F32),
-            jax.ShapeDtypeStruct(master.shape, F32),
-            jax.ShapeDtypeStruct((count, 4 * HD), BF16),
-        ),
-        in_specs=[pl.BlockSpec(memory_space=pltpu.SMEM), vmem, vmem, vmem, vmem, vmem],
-        out_specs=(vmem, vmem, vmem),
+        out_shape=outs,
+        in_specs=[anywhere] * 6,
+        out_specs=(anywhere,) * 3,
         scratch_shapes=scratch,
         compiler_params=pltpu.CompilerParams(
-            collective_id=0, has_side_effects=True, vmem_limit_bytes=48 * 1024 * 1024
+            collective_id=0, has_side_effects=True, vmem_limit_bytes=60 * 1024 * 1024
         ),
     )(bucket_table, master, momentum, gradient, tokens, norm_gain.reshape(-1, HD))
+    return pl.pallas_call(
+        hand_over,
+        out_shape=outs,
+        in_specs=[anywhere] * 3,
+        out_specs=(anywhere,) * 3,
+        scratch_shapes=[dma((3,))],
+    )(*made)
 
 
 def solution(mesh):

time: 86.5 us -> 105 us (1.21)
  Pallas kernels: 78 us -> 104 us
  local copies, waits for them, and re-layouts: 7.59 us -> 0 us
    pallas_call x1 -> x2, Pallas kernels: 78 us -> 104 us  [the longest x1 79.3 us: per_device(): pl.pallas_call(functools.partial(kernel, n, d_model), out_shape=outs, in_...]
    unnamed x15 -> x0, local copies, waits for them, and re-layouts: 7.59 us -> none
where the time goes in v2:
time: 105 us
  Pallas kernels  104 us (99%)
    pallas_call x1, Pallas kernels, per_device(): pl.pallas_call(functools.partial(kernel, n, d_model), out_shape=outs, in_...  79.3 us
    pallas_call x1, Pallas kernels, per_device(): pl.pallas_call(hand_over, out_shape=outs, in_specs=[anywhere] * 3, out_sp...  25 us

profile of v2, /device:TPU:1, one launch (start us, length us, event | category | flops | bytes accessed | tf_op | source)
XLA Modules:
  0.0 104.9 jit_solution(1713943969450191516)
XLA Ops:
  0.6 79.3 %shard_map.85 = (f32[2,64,512]{2,1,0:T(8,128)}, f32[2,64,512]{2,1,0:T(8,128)}, bf16[256,512]{1,0:T(8,128)(2,1)}) custom-call(s32[1,8]{1,0:T(1,128)} %table_in.1, f32[2,64,512]{2,1,0:T(8,128)} %master_in.1, f32[2,64,512]{2,1,0:T(8,128)} %momentum_in.1, f32[2,64,512]{2,1,0:T(8,128)} %gradient_in.1, bf16[256,2048]{1,0:T(8,128)(2,1)} %tokens_in.1, f32[64,128]{1,0:T(8,128)} %bitcast.1), custom_call_target="tpu_custom_call" | custom-call | tf_op jit(solution)/shard_map/pallas_call | solution.py:535
  79.9 25.0 %shard_map.86 = (f32[2,64,512]{2,1,0:T(8,128)}, f32[2,64,512]{2,1,0:T(8,128)}, bf16[256,512]{1,0:T(8,128)(2,1)}) custom-call(f32[2,64,512]{2,1,0:T(8,128)} %get-tuple-element.6.refs_0_, f32[2,64,512]{2,1,0:T(8,128)} %get-tuple-element.7.refs_1_, bf16[256,512]{1,0:T(8,128)(2,1)} %get-tuple-element.8.refs_2_), custom_call_target="tpu_custom_call" | custom-call | tf_op jit(solution)/shard_map/pallas_call | solution.py:545

commit v3 on v2

--- a/solution.py
+++ b/solution.py
@@ -48,10 +48,10 @@
 
 
 def kernel(n, d_model, table_in, master_in, momentum_in, gradient_in, tokens_in, gain_in, new_master,
-           new_momentum, key_values, table, master, momentum, gradient, tokens, gain, load, store, update,
+           new_momentum, key_values, table, master, momentum, gradient, tokens, gain, load, update,
            stacked, other_rows, heads, other_heads, packed, came1, part, came2, gram, ortho, weights,
            came_tokens, squares, normed, total, kv_send, kv_blocks, pair_send, pair_recv, gram_send,
-           gram_recv, token_send, token_recv, first_send, first_recv, begin_send, begin_recv, ring_send,
+           gram_recv, token_send, token_recv, first_send, first_recv, ring_send,
            ring_recv):
     half = n // 2
     rows = PACKED // n
@@ -126,14 +126,12 @@
             lanes = slice(slot * HD, (slot + 1) * HD)
             g = gradient[layer, :, lanes]
             m = beta_momentum * momentum[layer, :, lanes] + g
-            momentum[layer, :, lanes] = m
+            new_momentum[layer, :, lanes] = m
             update[layer * 4 + slot] = g + beta_momentum * m
             if layer == 0:
                 heads[slot] = master[0, :, lanes]
     for s in range(8):
         stacked[s] = update[held[s]]
-    stores = [pltpu.make_async_copy(momentum, new_momentum, store.at[0])]
-    stores[0].start()
 
     pl.semaphore_wait(barrier, len(greeted))
 
@@ -283,65 +281,66 @@
     slot_of = {o % n: k for k, o in enumerate(order)}
     ring_axis = (Z, Y)
 
-    def rsem(net, way, s, h):
-        return ring_send.at[net, way, s, h], ring_recv.at[net, way, s, h]
-
-    def bsem(net, way, k):
-        return begin_send.at[net, way, k], begin_recv.at[net, way, k]
+    near = n // 4
+    groups = ((0, 1), (1, 2 * near + 1), (2 * near + 1, n))
+
+    def rsem(net, way, s, g):
+        return ring_send.at[net, way, s, g], ring_recv.at[net, way, s, g]
 
     def fsem(net, k):
         return first_send.at[net, k], first_recv.at[net, k]
 
-    def sub(net, offset, h):
-        return weights.at[net, at(ring_axis[net], offset, n), pl.ds(h * half, half)]
-
-    def piece(net, offset, k):
-        return weights.at[net, at(ring_axis[net], offset, n), k]
-
-    def goes(way, s, h):
-        return s + 1 < half or way == h
-
-    def pass_on(net, j):
-        axis = axes[net][0]
-        if j + 1 < half:
-            for sign in (1, -1):
-                k = slot_of[sign * (j + 1) % n]
-                send(piece(net, 0, slot_of[sign * j % n]), piece(net, 0, k), fsem(net, k),
-                     {axis: at(axis, -sign, n)})
-        elif j + 1 == half:
-            k = slot_of[half]
-            source = jnp.where(c == 0, slot_of[j % n], slot_of[-j % n])
-            send(piece(net, 0, source), piece(net, 0, k), fsem(net, k), {axis: at(axis, 2 * c - 1, n)})
-
-    def begin(net, j):
-        for k in sorted({slot_of[j % n], slot_of[-j % n]}):
-            for way, sign in enumerate((1, -1)):
-                if goes(way, 0, k // half):
-                    moving = piece(net, 0, k)
-                    send(moving, moving, bsem(net, way, k),
-                         {ring_axis[net]: at(ring_axis[net], sign, n)})
+    def sub(net, offset, g):
+        low, high = groups[g]
+        return weights.at[net, at(ring_axis[net], offset, n), pl.ds(low, high - low)]
+
+    def piece(net, k):
+        return weights.at[net, place[ring_axis[net]], k]
+
+    def give(net, target, source, to):
+        k = slot_of[target % n]
+        send(piece(net, source), piece(net, k), fsem(net, k), {axes[net][0]: at(axes[net][0], to, n)})
+
+    def give_near(net):
+        for t in range(1, near + 1):
+            give(net, t, 0, -t)
+            give(net, -t, 0, t)
+
+    def give_far(net):
+        ahead, behind = slot_of[near % n], slot_of[-near % n]
+        for t in range(near + 1, half):
+            give(net, t, ahead, near - t)
+            give(net, -t, behind, t - near)
+        give(net, half, jnp.where(c == 0, ahead, behind), (2 * c - 1) * (half - near))
+
+    def first_came(net, g):
+        for k in range(*groups[g]):
+            arrived(piece(net, k), fsem(net, k), {axes[net][0]: at(axes[net][0], 1, n)})
+
+    def goes(way, s, g):
+        low, high = groups[g]
+        return low < high and (s + 1 < half or way == g % 2)
 
     seen = set()
 
-    def need(net, way, s, h):
-        if (net, way, s, h) in seen or not goes(way, s, h):
+    def need(net, way, s, g):
+        if (net, way, s, g) in seen or not goes(way, s, g):
             return
-        seen.add((net, way, s, h))
+        seen.add((net, way, s, g))
         sign = 1 if way == 0 else -1
-        to = {ring_axis[net]: at(ring_axis[net], sign, n)}
-        if s == 0:
-            for k in range(h * half, (h + 1) * half):
-                arrived(piece(net, -sign, k), bsem(net, way, k), to)
-        else:
-            arrived(sub(net, -sign * (s + 1), h), rsem(net, way, s, h), to)
-
-    def ring(s, h):
+        arrived(sub(net, -sign * (s + 1), g), rsem(net, way, s, g),
+                {ring_axis[net]: at(ring_axis[net], sign, n)})
+
+    def ring(s, g):
+        if s >= half:
+            return
         for net in range(2):
             for way, sign in enumerate((1, -1)):
-                if goes(way, s, h):
-                    need(net, way, s - 1, h)
-                    moving = sub(net, -sign * s, h)
-                    send(moving, moving, rsem(net, way, s, h),
+                if goes(way, s, g):
+                    if s > 0:
+                        need(net, way, s - 1, g)
+                    moving = sub(net, -sign * s, g)
+                    send(moving, moving, rsem(net, way, s, g),
                          {ring_axis[net]: at(ring_axis[net], sign, n)})
 
     for net in range(2):
@@ -349,23 +348,21 @@
         block = place[ring_axis[net]]
         weights[net, block, 0, c] = (heads[2 * c + net] - ortho[where, c]).astype(BF16)
         weights[net, block, 0, 1 - c] = (other_heads[net] - ortho[where, 1 - c]).astype(BF16)
-        pass_on(net, 0)
-        begin(net, 0)
-    for j in range(1, half + 1):
-        for net in range(2):
-            axis = axes[net][0]
-            for k in sorted({slot_of[j % n], slot_of[-j % n]}):
-                arrived(piece(net, 0, k), fsem(net, k), {axis: at(axis, 1, n)})
-            pass_on(net, j)
-            begin(net, j)
-        if j + 1 == half:
-            ring(1, 0)
+        give_near(net)
+    ring(0, 0)
+    for net in range(2):
+        first_came(net, 1)
+        give_far(net)
+    ring(0, 1)
 
     for i in range(8):
         lanes = slice((i % 4) * HD, (i % 4 + 1) * HD)
-        master[i // 4, :, lanes] = master[i // 4, :, lanes] - ortho[position[i], c]
-    stores.append(pltpu.make_async_copy(master, new_master, store.at[1]))
-    stores[1].start()
+        new_master[i // 4, :, lanes] = master[i // 4, :, lanes] - ortho[position[i], c]
+    ring(1, 0)
+    for net in range(2):
+        first_came(net, 2)
+    ring(0, 2)
+    ring(2, 0)
 
     def inverse_rms():
         mean = jnp.sum(squares[...], axis=1, keepdims=True) / d_model
@@ -392,15 +389,16 @@
         first = at(X, offset, 4) * blocks
         arrived(normed.at[pl.ds(first, blocks), 1 - c], pair(3 + k), partner)
 
-    def multiply(net, offset, fresh=False):
+    def multiply(net, offset, low=0, high=n, fresh=False):
         block = at(ring_axis[net], offset, n)
         axis = axes[net][0]
         wide = []
-        for o in order:
+        for o in order[low:high]:
             across = at(axis, o, n)
             feature = block * n + across if net == 0 else across * n + block
             wide.append(normed[feature].reshape(2 * count, HD))
-        product = dot(jnp.concatenate(wide, axis=1), weights[net, block].reshape(n * HD, HD))
+        rhs = weights[net, block, low:high].reshape((high - low) * HD, HD)
+        product = dot(jnp.concatenate(wide, axis=1), rhs)
         total[net] = product if fresh else total[net] + product
 
     def tokens_one():
@@ -421,55 +419,45 @@
         for k, offset in enumerate((0, -1, 1, 2)):
             partner_normed(offset, k)
         for net in range(2):
-            multiply(net, 0, True)
+            multiply(net, 0, fresh=True)
 
     def distance(k):
         for net in range(2):
-            for h in range(2):
+            for g in range(3):
                 for way in range(2):
-                    need(net, way, k - 1, h)
+                    need(net, way, k - 1, g)
             multiply(net, k)
-            if k < half:
-                multiply(net, -k)
+            multiply(net, -k)
 
     work = [
-        [tokens_one],
-        [tokens_three, tokens_two],
-        [lambda: normalise(tokens, 0, 0), lambda: normalise(came_tokens.at[0], -1, 1)],
-        [lambda: normalise(came_tokens.at[2], 1, 2), lambda: normalise(came_tokens.at[1], 2, 3)],
-        [own_block, functools.partial(distance, 1)],
+        (lambda: ring(1, 1), tokens_one),
+        (lambda: ring(3, 0), tokens_three, tokens_two),
+        (lambda: ring(1, 2), lambda: normalise(tokens, 0, 0), lambda: normalise(came_tokens.at[0], -1, 1)),
+        (lambda: ring(2, 1), lambda: normalise(came_tokens.at[2], 1, 2),
+         lambda: normalise(came_tokens.at[1], 2, 3)),
+        (lambda: ring(2, 2), own_block),
+        (lambda: ring(3, 1), lambda: ring(3, 2)),
     ]
-    work += [[functools.partial(distance, k)] for k in range(2, half + 1)]
-    steps = [(s, h) for s in range(1, half) for h in range(2) if (s, h) != (1, 0)]
-    for s, h in steps:
-        for task in work.pop(0):
-            task()
-        ring(s, h)
     for tasks in work:
         for task in tasks:
             task()
-
-    for net in range(2):
+    for k in range(1, half):
+        distance(k)
+
+    for net in range(2):
+        for g in (0, 1, 2):
+            for way in range(2):
+                need(net, way, half - 1, g)
+        multiply(net, half)
         kv_send[net] = total[net, pl.ds(pl.multiple_of((1 - c) * count, 16), count)].astype(BF16)
-    send(kv_send, kv_blocks.at[pl.ds(2 * c, 2)], pair(7), partner)
+        send(kv_send.at[net], kv_blocks.at[2 * c + net], pair(7 + net), partner)
     for net in range(2):
         kv_blocks[2 * c + net] = total[net, pl.ds(pl.multiple_of(c * count, 16), count)].astype(BF16)
-
-    def store_columns(core, k):
-        for net in range(2):
-            block = 2 * core + net
-            lanes = pl.ds(pl.multiple_of(block * HD, HD), HD)
-            stores.append(
-                pltpu.make_async_copy(kv_blocks.at[block], key_values.at[:, lanes], store.at[k + net])
-            )
-            stores[-1].start()
-
-    store_columns(c, 2)
     finish_sends()
-    arrived(kv_blocks.at[pl.ds(2 * (1 - c), 2)], pair(7), partner)
-    store_columns(1 - c, 4)
-    for copy in stores:
-        copy.wait()
+    for net in range(2):
+        arrived(kv_blocks.at[2 * (1 - c) + net], pair(7 + net), partner)
+    for k in range(4):
+        key_values[:, k * HD : (k + 1) * HD] = kv_blocks[k]
 
 
 def hand_over(*refs):
@@ -487,14 +475,13 @@
     blocks = width // HD
     rows = PACKED // n
     half = n // 2
-    anywhere = pl.BlockSpec(memory_space=pl.ANY)
+    hbm, anywhere, vmem = (pl.BlockSpec(memory_space=m) for m in (pltpu.HBM, pl.ANY, pltpu.VMEM))
     dma = pltpu.SemaphoreType.DMA
     scratch = [
         pltpu.SMEM(bucket_table.shape, jnp.int32),
         *[pltpu.VMEM(master.shape, F32) for _ in range(3)],
         pltpu.VMEM(tokens.shape, BF16),
         pltpu.VMEM((4 * blocks, HD), F32),
-        dma((6,)),
         dma((6,)),
         pltpu.VMEM((8, height, HD), F32),
         pltpu.VMEM((8, height, HD), F32),
@@ -514,18 +501,16 @@
         pltpu.VMEM((2, 2 * count, HD), F32),
         pltpu.VMEM((2, count, HD), BF16),
         pltpu.VMEM((4, count, HD), BF16),
-        dma((8,)),
-        dma((8,)),
+        dma((9,)),
+        dma((9,)),
         dma((3, 2, n - 1)),
         dma((3, 2, n - 1)),
         dma((6,)),
         dma((6,)),
         dma((2, n)),
         dma((2, n)),
-        dma((2, 2, n)),
-        dma((2, 2, n)),
-        dma((2, 2, half, 2)),
-        dma((2, 2, half, 2)),
+        dma((2, 2, half, 3)),
+        dma((2, 2, half, 3)),
     ]
     outs = (
         jax.ShapeDtypeStruct(master.shape, F32),
@@ -535,19 +520,23 @@
     made = pl.pallas_call(
         functools.partial(kernel, n, d_model),
         out_shape=outs,
-        in_specs=[anywhere] * 6,
-        out_specs=(anywhere,) * 3,
+        in_specs=[hbm] * 6,
+        out_specs=(vmem,) * 3,
         scratch_shapes=scratch,
         compiler_params=pltpu.CompilerParams(
-            collective_id=0, has_side_effects=True, vmem_limit_bytes=60 * 1024 * 1024
+            collective_id=0, has_side_effects=True, vmem_limit_bytes=48 * 1024 * 1024
         ),
-    )(bucket_table, master, momentum, gradient, tokens, norm_gain.reshape(-1, HD))
+    )(*(
+        pltpu.with_memory_space_constraint(a, pltpu.HBM)
+        for a in (bucket_table, master, momentum, gradient, tokens, norm_gain.reshape(-1, HD))
+    ))
     return pl.pallas_call(
         hand_over,
         out_shape=outs,
-        in_specs=[anywhere] * 3,
-        out_specs=(anywhere,) * 3,
+        in_specs=[vmem] * 3,
+        out_specs=(hbm,) * 3,
         scratch_shapes=[dma((3,))],
+        compiler_params=pltpu.CompilerParams(vmem_limit_bytes=4 * 1024 * 1024),
     )(*made)
 
 

time: 105 us -> 77.2 us (0.74)
  Pallas kernels: 104 us -> 76.4 us
    pallas_call x1, Pallas kernels: 25 us -> 0.9 us  [per_device(): pl.pallas_call(hand_over, out_shape=outs, in_specs=[vmem] * 3, out_specs=...]
    pallas_call x1, Pallas kernels: 79.3 us -> 75.5 us  [per_device(): pl.pallas_call(functools.partial(kernel, n, d_model), out_shape=outs, in_...]
where the time goes in v3:
time: 77.2 us; the launch traced here: 77.1 us
  Pallas kernels  76.4 us (99%)
    pallas_call x1, Pallas kernels, per_device(): pl.pallas_call(functools.partial(kernel, n, d_model), out_shape=outs, in_...  75.5 us

profile of v3, /device:TPU:1, one launch (start us, length us, event | category | flops | bytes accessed | tf_op | source)
XLA Modules:
  0.0 77.1 jit_solution(4520455041105248168)
XLA Ops:
  0.6 75.5 %shard_map.85 = (f32[2,64,512]{2,1,0:T(8,128)S(1)}, f32[2,64,512]{2,1,0:T(8,128)S(1)}, bf16[256,512]{1,0:T(8,128)(2,1)S(1)}) custom-call(s32[1,8]{1,0:T(1,128)} %table_in.1, f32[2,64,512]{2,1,0:T(8,128)} %master_in.1, f32[2,64,512]{2,1,0:T(8,128)} %momentum_in.1, f32[2,64,512]{2,1,0:T(8,128)} %gradient_in.1, bf16[256,2048]{1,0:T(8,128)(2,1)} %tokens_in.1, ...), custom_call_target="tpu_custom_call" | custom-call | tf_op jit(solution)/shard_map/pallas_call | solution.py:520
  76.2 0.9 %shard_map.86 = (f32[2,64,512]{2,1,0:T(8,128)}, f32[2,64,512]{2,1,0:T(8,128)}, bf16[256,512]{1,0:T(8,128)(2,1)}) custom-call(f32[2,64,512]{2,1,0:T(8,128)S(1)} %get-tuple-element.6.refs_0_, f32[2,64,512]{2,1,0:T(8,128)S(1)} %get-tuple-element.7.refs_1_, bf16[256,512]{1,0:T(8,128)(2,1)S(1)} %get-tuple-element.8.refs_2_), custom_call_target="tpu_custom_call" | custom-call | tf_op jit(solution)/shard_map/pallas_call | solution.py:533

commit v4 on v3

--- a/solution.py
+++ b/solution.py
@@ -81,8 +81,8 @@
             device_id=to, device_id_type=pl.DeviceIdType.MESH,
         ).wait_recv()
 
-    def finish_sends():
-        while pending:
+    def settle(keep):
+        while len(pending) > keep:
             pending.pop(0).wait_send()
 
     partner = {C: 1 - c}
@@ -162,13 +162,20 @@
         other = jnp.concatenate([other_rows[2 * b], other_rows[2 * b + 1]], axis=1)
         return jnp.concatenate([own, other], axis=0)
 
-    def lines(ref, net, chunk):
-        return ref.at[net, pl.ds(pl.multiple_of(chunk * rows, 8), rows)]
+    parts = ((0, 16), (16, rows))
+
+    def lines(ref, net, chunk, p):
+        low, high = parts[p]
+        return ref.at[net, pl.ds(pl.multiple_of(chunk * rows + low, 8), high - low)]
+
+    def some(ref, net, d, p):
+        low, high = parts[p]
+        return ref.at[net, d - 1, pl.ds(low, high - low)]
 
     far_first = [o % n for o in reversed(near_first(n)[1:])]
 
-    def gsem(stage, net, d):
-        return gram_send.at[stage, net, d - 1], gram_recv.at[stage, net, d - 1]
+    def gsem(stage, net, p, d):
+        return gram_send.at[stage, net, p, d - 1], gram_recv.at[stage, net, p, d - 1]
 
     r_id = lax.broadcasted_iota(jnp.int32, (HD, HD), 0)
     c_id = lax.broadcasted_iota(jnp.int32, (HD, HD), 1)
@@ -180,10 +187,12 @@
         packed[net, HD : 2 * HD] = g[:HD, HD:]
         diagonal = jnp.sum(jnp.where(r_id == c_id, second, 0.0), axis=0, keepdims=True)
         packed[net, 2 * HD :] = jnp.broadcast_to(diagonal, (PACKED - 2 * HD, HD))
-        axis = axes[net][0]
-        for d in far_first:
-            to = at(axis, d, n)
-            send(lines(packed, net, to), came1.at[net, d - 1], gsem(0, net, d), {axis: to})
+    for p in range(2):
+        for net in range(2):
+            axis = axes[net][0]
+            for d in far_first:
+                to = at(axis, d, n)
+                send(lines(packed, net, to, p), some(came1, net, d, p), gsem(0, net, p, d), {axis: to})
 
     def add_squares(src, fresh):
         tile = 32 if count % 32 == 0 else 16
@@ -201,27 +210,30 @@
 
     add_squares(tokens, True)
 
-    for net in range(2):
-        axis, other = axes[net]
-        for d in range(1, n):
-            arrived(came1.at[net, d - 1], gsem(0, net, d), {axis: at(axis, d, n)})
-        s = packed[net, pl.ds(pl.multiple_of(place[axis] * rows, 8), rows)]
-        for d in range(1, n):
-            s = s + came1[net, d - 1]
-        part[net] = s
-        for d in far_first:
-            send(part.at[net], came2.at[net, d - 1], gsem(1, net, d), {other: at(other, d, n)})
-    for net in range(2):
-        axis, other = axes[net]
-        for d in range(1, n):
-            arrived(came2.at[net, d - 1], gsem(1, net, d), {other: at(other, d, n)})
-        s = part[net]
-        for d in range(1, n):
-            s = s + came2[net, d - 1]
-        gram[net, pl.ds(pl.multiple_of(place[axis] * rows, 8), rows)] = s
-        own = lines(gram, net, place[axis])
-        for d in far_first:
-            send(own, own, gsem(2, net, d), {axis: at(axis, d, n)})
+    for p, (low, high) in enumerate(parts):
+        for net in range(2):
+            axis, other = axes[net]
+            for d in range(1, n):
+                arrived(some(came1, net, d, p), gsem(0, net, p, d), {axis: at(axis, d, n)})
+            t = lines(packed, net, place[axis], p)[...]
+            for d in range(1, n):
+                t = t + came1[net, d - 1, low:high]
+            part[net, low:high] = t
+            for d in far_first:
+                send(part.at[net, pl.ds(low, high - low)], some(came2, net, d, p), gsem(1, net, p, d),
+                     {other: at(other, d, n)})
+    for p, (low, high) in enumerate(parts):
+        for net in range(2):
+            axis, other = axes[net]
+            for d in range(1, n):
+                arrived(some(came2, net, d, p), gsem(1, net, p, d), {other: at(other, d, n)})
+            t = part[net, low:high]
+            for d in range(1, n):
+                t = t + came2[net, d - 1, low:high]
+            own = lines(gram, net, place[axis], p)
+            own[...] = t
+            for d in far_first:
+                send(own, own, gsem(2, net, p, d), {axis: at(axis, d, n)})
 
     arrived(came_tokens.at[0, upper], tok(0), right)
     send(came_tokens.at[0, upper], came_tokens.at[1, upper], tok(4), right)
@@ -230,8 +242,9 @@
 
     for net in range(2):
         axis = axes[net][0]
-        for d in range(1, n):
-            arrived(lines(gram, net, at(axis, -d, n)), gsem(2, net, d), {axis: at(axis, d, n)})
+        for p in range(2):
+            for d in range(1, n):
+                arrived(lines(gram, net, at(axis, -d, n), p), gsem(2, net, p, d), {axis: at(axis, d, n)})
 
     eye = jnp.where(
         lax.broadcasted_iota(jnp.int32, (2 * HD, 2 * HD), 0)
@@ -272,10 +285,11 @@
             lanes = slice(h * HD, (h + 1) * HD)
             ortho[4 * c + 2 * net + h, c] = moved[:height, lanes]
             ortho[4 * c + 2 * net + h, 1 - c] = moved[height:, lanes]
-    mine = ortho.at[pl.ds(4 * c, 4)]
-    send(mine, mine, pair(2), partner)
+        mine = ortho.at[pl.ds(4 * c + 2 * net, 2)]
+        send(mine, mine, pair((2, 9)[net]), partner)
     arrived(other_heads, pair(1), partner)
-    arrived(ortho.at[pl.ds(4 * (1 - c), 4)], pair(2), partner)
+    for net in range(2):
+        arrived(ortho.at[pl.ds(4 * (1 - c) + 2 * net, 2)], pair((2, 9)[net]), partner)
 
     order = near_first(n)
     slot_of = {o % n: k for k, o in enumerate(order)}
@@ -430,11 +444,11 @@
             multiply(net, -k)
 
     work = [
-        (lambda: ring(1, 1), tokens_one),
-        (lambda: ring(3, 0), tokens_three, tokens_two),
+        (lambda: ring(1, 1), tokens_one, lambda: settle(40)),
+        (lambda: ring(3, 0), tokens_three, tokens_two, lambda: settle(30)),
         (lambda: ring(1, 2), lambda: normalise(tokens, 0, 0), lambda: normalise(came_tokens.at[0], -1, 1)),
         (lambda: ring(2, 1), lambda: normalise(came_tokens.at[2], 1, 2),
-         lambda: normalise(came_tokens.at[1], 2, 3)),
+         lambda: normalise(came_tokens.at[1], 2, 3), lambda: settle(24)),
         (lambda: ring(2, 2), own_block),
         (lambda: ring(3, 1), lambda: ring(3, 2)),
     ]
@@ -443,6 +457,8 @@
             task()
     for k in range(1, half):
         distance(k)
+        if k + 1 < half:
+            settle(14)
 
     for net in range(2):
         for g in (0, 1, 2):
@@ -453,7 +469,7 @@
         send(kv_send.at[net], kv_blocks.at[2 * c + net], pair(7 + net), partner)
     for net in range(2):
         kv_blocks[2 * c + net] = total[net, pl.ds(pl.multiple_of(c * count, 16), count)].astype(BF16)
-    finish_sends()
+    settle(0)
     for net in range(2):
         arrived(kv_blocks.at[2 * (1 - c) + net], pair(7 + net), partner)
     for k in range(4):
@@ -501,10 +517,10 @@
         pltpu.VMEM((2, 2 * count, HD), F32),
         pltpu.VMEM((2, count, HD), BF16),
         pltpu.VMEM((4, count, HD), BF16),
-        dma((9,)),
-        dma((9,)),
-        dma((3, 2, n - 1)),
-        dma((3, 2, n - 1)),
+        dma((10,)),
+        dma((10,)),
+        dma((3, 2, 2, n - 1)),
+        dma((3, 2, 2, n - 1)),
         dma((6,)),
         dma((6,)),
         dma((2, n)),

time: 77.2 us -> 75.6 us (0.979)
  Pallas kernels: 76.4 us -> 74.8 us
    pallas_call x1, Pallas kernels: 75.5 us -> 73.9 us  [per_device(): pl.pallas_call(functools.partial(kernel, n, d_model), out_shape=outs, in_...]
where the time goes in v4:
time: 75.6 us; the launch traced here: 75.4 us
  Pallas kernels  74.8 us (99%)
    pallas_call x1, Pallas kernels, per_device(): pl.pallas_call(functools.partial(kernel, n, d_model), out_shape=outs, in_...  73.9 us

profile of v4, /device:TPU:1, one launch (start us, length us, event | category | flops | bytes accessed | tf_op | source)
XLA Modules:
  0.0 75.4 jit_solution(12136603752292940343)
XLA Ops:
  0.6 73.9 %shard_map.85 = (f32[2,64,512]{2,1,0:T(8,128)S(1)}, f32[2,64,512]{2,1,0:T(8,128)S(1)}, bf16[256,512]{1,0:T(8,128)(2,1)S(1)}) custom-call(s32[1,8]{1,0:T(1,128)} %table_in.1, f32[2,64,512]{2,1,0:T(8,128)} %master_in.1, f32[2,64,512]{2,1,0:T(8,128)} %momentum_in.1, f32[2,64,512]{2,1,0:T(8,128)} %gradient_in.1, bf16[256,2048]{1,0:T(8,128)(2,1)} %tokens_in.1, ...), custom_call_target="tpu_custom_call" | custom-call | tf_op jit(solution)/shard_map/pallas_call | solution.py:536
  74.5 0.9 %shard_map.86 = (f32[2,64,512]{2,1,0:T(8,128)}, f32[2,64,512]{2,1,0:T(8,128)}, bf16[256,512]{1,0:T(8,128)(2,1)}) custom-call(f32[2,64,512]{2,1,0:T(8,128)S(1)} %get-tuple-element.6.refs_0_, f32[2,64,512]{2,1,0:T(8,128)S(1)} %get-tuple-element.7.refs_1_, bf16[256,512]{1,0:T(8,128)(2,1)S(1)} %get-tuple-element.8.refs_2_), custom_call_target="tpu_custom_call" | custom-call | tf_op jit(solution)/shard_map/pallas_call | solution.py:549

commit v5 on v4

--- a/solution.py
+++ b/solution.py
@@ -50,8 +50,8 @@
 def kernel(n, d_model, table_in, master_in, momentum_in, gradient_in, tokens_in, gain_in, new_master,
            new_momentum, key_values, table, master, momentum, gradient, tokens, gain, load, update,
            stacked, other_rows, heads, other_heads, packed, came1, part, came2, gram, ortho, weights,
-           came_tokens, squares, normed, total, kv_send, kv_blocks, pair_send, pair_recv, gram_send,
-           gram_recv, token_send, token_recv, first_send, first_recv, ring_send,
+           came_tokens, squares, normed, total, pair_send, pair_recv, gram_send,
+           gram_recv, token_send, token_recv, first_send, first_recv, core_send, core_recv, ring_send,
            ring_recv):
     half = n // 2
     rows = PACKED // n
@@ -61,7 +61,7 @@
     z, y, c, x = (lax.axis_index(a) for a in (Z, Y, C, X))
     axes = ((Y, Z), (Z, Y))
     place = {Y: y, Z: z}
-    pending = []
+    sent, ended = [], [0]
 
     def at(axis, offset, size):
         here = {Y: y, Z: z, X: x}[axis]
@@ -73,7 +73,7 @@
             device_id=to, device_id_type=pl.DeviceIdType.MESH,
         )
         copy.start()
-        pending.append(copy)
+        sent.append(copy)
 
     def arrived(ref, sems, to):
         pltpu.make_async_remote_copy(
@@ -81,9 +81,10 @@
             device_id=to, device_id_type=pl.DeviceIdType.MESH,
         ).wait_recv()
 
-    def settle(keep):
-        while len(pending) > keep:
-            pending.pop(0).wait_send()
+    def settle(mark):
+        for copy in sent[ended[0] : mark]:
+            copy.wait_send()
+        ended[0] = max(ended[0], mark)
 
     partner = {C: 1 - c}
 
@@ -250,7 +251,8 @@
         lax.broadcasted_iota(jnp.int32, (2 * HD, 2 * HD), 0)
         == lax.broadcasted_iota(jnp.int32, (2 * HD, 2 * HD), 1), 1.0, 0.0
     ).astype(F32)
-    grams, scales, products = [], [], [None, None]
+    step = learn_rate * math.sqrt(max(1.0, d_model / (2.0 * HD)))
+    grams, ortho_rows = [], []
     for net in range(2):
         both, corner = gram[net, 0:HD], gram[net, HD : 2 * HD]
         turned = both.T
@@ -262,7 +264,7 @@
         trace = jnp.sum(jnp.sum(g * eye, axis=1, keepdims=True), axis=0, keepdims=True)
         scale = 1.0 / (jnp.sqrt(trace) + frob_epsilon)
         grams.append(g * (scale * scale))
-        scales.append(scale)
+        ortho_rows.append(chip_rows(net) * scale)
     for iteration in range(NS_ITERS):
         gs = [split(g) for g in grams]
         squared = [dot3(g, g) for g in gs]
@@ -270,26 +272,22 @@
             first_coeff * eye + (cube_coeff * g + fifth_coeff * q) for g, q in zip(grams, squared)
         ]
         fs = [split(f) for f in factor]
-        if iteration == 0:
-            products = factor
-        else:
-            products = [dot3(split(p), f) for p, f in zip(products, fs)]
         if iteration + 1 < NS_ITERS:
             half_way = [dot3(f, g) for f, g in zip(fs, gs)]
             grams = [dot3(split(h), f) for h, f in zip(half_way, fs)]
-
-    step = learn_rate * math.sqrt(max(1.0, d_model / (2.0 * HD)))
-    for net in range(2):
-        moved = dot3(split(chip_rows(net)), split(products[net] * (scales[net] * step)))
+            ortho_rows = [dot3(split(o), f) for o, f in zip(ortho_rows, fs)]
+
+    for net in range(2):
+        moved = dot3(split(ortho_rows[net]), fs[net]) * step
         for h in range(2):
             lanes = slice(h * HD, (h + 1) * HD)
             ortho[4 * c + 2 * net + h, c] = moved[:height, lanes]
             ortho[4 * c + 2 * net + h, 1 - c] = moved[height:, lanes]
         mine = ortho.at[pl.ds(4 * c + 2 * net, 2)]
-        send(mine, mine, pair((2, 9)[net]), partner)
+        send(mine, mine, pair(2 + net), partner)
     arrived(other_heads, pair(1), partner)
     for net in range(2):
-        arrived(ortho.at[pl.ds(4 * (1 - c) + 2 * net, 2)], pair((2, 9)[net]), partner)
+        arrived(ortho.at[pl.ds(4 * (1 - c) + 2 * net, 2)], pair(2 + net), partner)
 
     order = near_first(n)
     slot_of = {o % n: k for k, o in enumerate(order)}
@@ -304,12 +302,12 @@
     def fsem(net, k):
         return first_send.at[net, k], first_recv.at[net, k]
 
-    def sub(net, offset, g):
+    def sub(net, offset, g, core=c):
         low, high = groups[g]
-        return weights.at[net, at(ring_axis[net], offset, n), pl.ds(low, high - low)]
+        return weights.at[core, net, at(ring_axis[net], offset, n), pl.ds(low, high - low)]
 
     def piece(net, k):
-        return weights.at[net, place[ring_axis[net]], k]
+        return weights.at[c, net, place[ring_axis[net]], k]
 
     def give(net, target, source, to):
         k = slot_of[target % n]
@@ -328,8 +326,26 @@
         give(net, half, jnp.where(c == 0, ahead, behind), (2 * c - 1) * (half - near))
 
     def first_came(net, g):
+        if groups[g][0] < groups[g][1]:
+            fresh.append((net, 0, g))
         for k in range(*groups[g]):
             arrived(piece(net, k), fsem(net, k), {axes[net][0]: at(axes[net][0], 1, n)})
+
+    def csem(net, offset, g):
+        return core_send.at[net, offset % n, g], core_recv.at[net, offset % n, g]
+
+    fresh = []
+
+    def share():
+        while fresh:
+            net, offset, g = fresh.pop(0)
+            moving = sub(net, offset, g)
+            send(moving, moving, csem(net, offset, g), partner)
+
+    def shared(net, offset):
+        for g, (low, high) in enumerate(groups):
+            if low < high:
+                arrived(sub(net, offset, g, 1 - c), csem(net, offset, g), partner)
 
     def goes(way, s, g):
         low, high = groups[g]
@@ -344,6 +360,7 @@
         sign = 1 if way == 0 else -1
         arrived(sub(net, -sign * (s + 1), g), rsem(net, way, s, g),
                 {ring_axis[net]: at(ring_axis[net], sign, n)})
+        fresh.append((net, -sign * (s + 1), g))
 
     def ring(s, g):
         if s >= half:
@@ -356,18 +373,22 @@
                     moving = sub(net, -sign * s, g)
                     send(moving, moving, rsem(net, way, s, g),
                          {ring_axis[net]: at(ring_axis[net], sign, n)})
-
+        share()
+
+    marks = [len(sent)]
     for net in range(2):
         where = jnp.where(c == 0, position[net], position[2 + net])
         block = place[ring_axis[net]]
-        weights[net, block, 0, c] = (heads[2 * c + net] - ortho[where, c]).astype(BF16)
-        weights[net, block, 0, 1 - c] = (other_heads[net] - ortho[where, 1 - c]).astype(BF16)
+        weights[c, net, block, 0, c] = (heads[2 * c + net] - ortho[where, c]).astype(BF16)
+        weights[c, net, block, 0, 1 - c] = (other_heads[net] - ortho[where, 1 - c]).astype(BF16)
         give_near(net)
+        fresh.append((net, 0, 0))
     ring(0, 0)
     for net in range(2):
         first_came(net, 1)
         give_far(net)
     ring(0, 1)
+    marks.append(len(sent))
 
     for i in range(8):
         lanes = slice((i % 4) * HD, (i % 4 + 1) * HD)
@@ -382,7 +403,7 @@
         mean = jnp.sum(squares[...], axis=1, keepdims=True) / d_model
         squares[...] = jnp.broadcast_to(lax.rsqrt(mean + rms_epsilon), squares.shape)
 
-    def normalise(src, offset, k):
+    def normalise(src, offset):
         tile = 32 if count % 32 == 0 else 16
         first = at(X, offset, 4) * blocks
 
@@ -392,28 +413,21 @@
             for j in range(blocks):
                 v = src[r, j * HD : (j + 1) * HD].astype(F32)
                 v = v * inverse * gain[pl.ds(first + j, 1), :]
-                normed[first + j, c, r] = v.astype(BF16)
+                normed[first + j, r] = v.astype(BF16)
             return 0
 
         lax.fori_loop(0, count // tile, body, 0)
-        made = normed.at[pl.ds(first, blocks), c]
-        send(made, made, pair(3 + k), partner)
-
-    def partner_normed(offset, k):
-        first = at(X, offset, 4) * blocks
-        arrived(normed.at[pl.ds(first, blocks), 1 - c], pair(3 + k), partner)
-
-    def multiply(net, offset, low=0, high=n, fresh=False):
+    def multiply(net, offset, first=False):
+        shared(net, offset)
         block = at(ring_axis[net], offset, n)
         axis = axes[net][0]
         wide = []
-        for o in order[low:high]:
+        for o in order:
             across = at(axis, o, n)
-            feature = block * n + across if net == 0 else across * n + block
-            wide.append(normed[feature].reshape(2 * count, HD))
-        rhs = weights[net, block, low:high].reshape((high - low) * HD, HD)
-        product = dot(jnp.concatenate(wide, axis=1), rhs)
-        total[net] = product if fresh else total[net] + product
+            wide.append(normed[block * n + across if net == 0 else across * n + block])
+        tall = [weights[core, net, block].reshape(n * HD, HD) for core in range(2)]
+        product = dot(jnp.concatenate(wide, axis=1), jnp.concatenate(tall, axis=1))
+        total[net] = product if first else total[net] + product
 
     def tokens_one():
         arrived(came_tokens.at[0, lower], tok(2), right)
@@ -430,50 +444,41 @@
         inverse_rms()
 
     def own_block():
-        for k, offset in enumerate((0, -1, 1, 2)):
-            partner_normed(offset, k)
-        for net in range(2):
-            multiply(net, 0, fresh=True)
+        for net in range(2):
+            multiply(net, 0, True)
 
     def distance(k):
         for net in range(2):
             for g in range(3):
                 for way in range(2):
                     need(net, way, k - 1, g)
+        share()
+        for net in range(2):
             multiply(net, k)
-            multiply(net, -k)
-
-    work = [
-        (lambda: ring(1, 1), tokens_one, lambda: settle(40)),
-        (lambda: ring(3, 0), tokens_three, tokens_two, lambda: settle(30)),
-        (lambda: ring(1, 2), lambda: normalise(tokens, 0, 0), lambda: normalise(came_tokens.at[0], -1, 1)),
-        (lambda: ring(2, 1), lambda: normalise(came_tokens.at[2], 1, 2),
-         lambda: normalise(came_tokens.at[1], 2, 3), lambda: settle(24)),
-        (lambda: ring(2, 2), own_block),
-        (lambda: ring(3, 1), lambda: ring(3, 2)),
-    ]
+            if k < half:
+                multiply(net, -k)
+
+    work = (
+        (lambda: ring(1, 1), tokens_one, lambda: settle(marks[0]), lambda: marks.append(len(sent))),
+        (lambda: ring(3, 0), tokens_three),
+        (lambda: ring(1, 2), tokens_two, lambda: normalise(tokens, 0), lambda: settle(marks[1])),
+        (lambda: ring(2, 1), lambda: marks.append(len(sent)), lambda: normalise(came_tokens.at[0], -1),
+         lambda: normalise(came_tokens.at[2], 1), lambda: normalise(came_tokens.at[1], 2)),
+        (lambda: ring(2, 2), own_block, functools.partial(distance, 1) if half > 1 else share),
+        (lambda: ring(3, 1), lambda: settle(marks[2]), lambda: ring(3, 2)),
+    )
     for tasks in work:
         for task in tasks:
             task()
-    for k in range(1, half):
+    for k in range(2, half):
         distance(k)
-        if k + 1 < half:
-            settle(14)
-
-    for net in range(2):
-        for g in (0, 1, 2):
-            for way in range(2):
-                need(net, way, half - 1, g)
-        multiply(net, half)
-        kv_send[net] = total[net, pl.ds(pl.multiple_of((1 - c) * count, 16), count)].astype(BF16)
-        send(kv_send.at[net], kv_blocks.at[2 * c + net], pair(7 + net), partner)
-    for net in range(2):
-        kv_blocks[2 * c + net] = total[net, pl.ds(pl.multiple_of(c * count, 16), count)].astype(BF16)
-    settle(0)
-    for net in range(2):
-        arrived(kv_blocks.at[2 * (1 - c) + net], pair(7 + net), partner)
-    for k in range(4):
-        key_values[:, k * HD : (k + 1) * HD] = kv_blocks[k]
+    settle(marks[3])
+    distance(half)
+    for net in range(2):
+        for core in range(2):
+            columns = slice((2 * core + net) * HD, (2 * core + net + 1) * HD)
+            key_values[:, columns] = total[net, :, core * HD : (core + 1) * HD].astype(BF16)
+    settle(len(sent))
 
 
 def hand_over(*refs):
@@ -510,21 +515,21 @@
         pltpu.VMEM((2, n - 1, rows, HD), F32),
         pltpu.VMEM((2, PACKED, HD), F32),
         pltpu.VMEM((8, 2, height, HD), F32),
-        pltpu.VMEM((2, n, n, 2, height, HD), BF16),
+        pltpu.VMEM((2, 2, n, n, 2, height, HD), BF16),
         pltpu.VMEM((3, count, width), BF16),
         pltpu.VMEM((count, HD), F32),
-        pltpu.VMEM((4 * blocks, 2, count, HD), BF16),
-        pltpu.VMEM((2, 2 * count, HD), F32),
-        pltpu.VMEM((2, count, HD), BF16),
-        pltpu.VMEM((4, count, HD), BF16),
-        dma((10,)),
-        dma((10,)),
+        pltpu.VMEM((4 * blocks, count, HD), BF16),
+        pltpu.VMEM((2, count, 2 * HD), F32),
+        dma((4,)),
+        dma((4,)),
         dma((3, 2, 2, n - 1)),
         dma((3, 2, 2, n - 1)),
         dma((6,)),
         dma((6,)),
         dma((2, n)),
         dma((2, n)),
+        dma((2, n, 3)),
+        dma((2, n, 3)),
         dma((2, 2, half, 3)),
         dma((2, 2, half, 3)),
     ]

time: 75.6 us -> 74.2 us (0.981)
  Pallas kernels: 74.8 us -> 73.4 us
    pallas_call x1, Pallas kernels: 73.9 us -> 72.5 us  [per_device(): pl.pallas_call(functools.partial(kernel, n, d_model), out_shape=outs, in_...]
where the time goes in v5:
time: 74.2 us; the launch traced here: 74 us
  Pallas kernels  73.4 us (99%)
    pallas_call x1, Pallas kernels, per_device(): pl.pallas_call(functools.partial(kernel, n, d_model), out_shape=outs, in_...  72.5 us

profile of v5, /device:TPU:1, one launch (start us, length us, event | category | flops | bytes accessed | tf_op | source)
XLA Modules:
  0.0 74.0 jit_solution(8692023035643479650)
XLA Ops:
  0.6 72.5 %shard_map.85 = (f32[2,64,512]{2,1,0:T(8,128)S(1)}, f32[2,64,512]{2,1,0:T(8,128)S(1)}, bf16[256,512]{1,0:T(8,128)(2,1)S(1)}) custom-call(s32[1,8]{1,0:T(1,128)} %table_in.1, f32[2,64,512]{2,1,0:T(8,128)} %master_in.1, f32[2,64,512]{2,1,0:T(8,128)} %momentum_in.1, f32[2,64,512]{2,1,0:T(8,128)} %gradient_in.1, bf16[256,2048]{1,0:T(8,128)(2,1)} %tokens_in.1, ...), custom_call_target="tpu_custom_call" | custom-call | tf_op jit(solution)/shard_map/pallas_call | solution.py:541
  73.1 0.9 %shard_map.86 = (f32[2,64,512]{2,1,0:T(8,128)}, f32[2,64,512]{2,1,0:T(8,128)}, bf16[256,512]{1,0:T(8,128)(2,1)}) custom-call(f32[2,64,512]{2,1,0:T(8,128)S(1)} %get-tuple-element.6.refs_0_, f32[2,64,512]{2,1,0:T(8,128)S(1)} %get-tuple-element.7.refs_1_, bf16[256,512]{1,0:T(8,128)(2,1)S(1)} %get-tuple-element.8.refs_2_), custom_call_target="tpu_custom_call" | custom-call | tf_op jit(solution)/shard_map/pallas_call | solution.py:554

commit v6 on v5

--- a/solution.py
+++ b/solution.py
@@ -349,7 +349,7 @@
 
     def goes(way, s, g):
         low, high = groups[g]
-        return low < high and (s + 1 < half or way == g % 2)
+        return low < high and (s + 1 < half or (way == 0) == (g == 2))
 
     seen = set()
 
@@ -362,6 +362,14 @@
                 {ring_axis[net]: at(ring_axis[net], sign, n)})
         fresh.append((net, -sign * (s + 1), g))
 
+    def skip_one():
+        for net in range(2):
+            for way, sign in enumerate((1, -1)):
+                if half > 2:
+                    own = sub(net, 0, 0)
+                    send(own, own, rsem(net, way, 1, 0),
+                         {ring_axis[net]: at(ring_axis[net], 2 * sign, n)})
+
     def ring(s, g):
         if s >= half:
             return
@@ -370,6 +378,8 @@
                 if goes(way, s, g):
                     if s > 0:
                         need(net, way, s - 1, g)
+                    if half > 2 and (s, g) == (1, 0):
+                        continue
                     moving = sub(net, -sign * s, g)
                     send(moving, moving, rsem(net, way, s, g),
                          {ring_axis[net]: at(ring_axis[net], sign, n)})
@@ -384,6 +394,7 @@
         give_near(net)
         fresh.append((net, 0, 0))
     ring(0, 0)
+    skip_one()
     for net in range(2):
         first_came(net, 1)
         give_far(net)
@@ -453,6 +464,8 @@
                 for way in range(2):
                     need(net, way, k - 1, g)
         share()
+        if k == half:
+            settle(len(sent))
         for net in range(2):
             multiply(net, k)
             if k < half:
@@ -478,7 +491,6 @@
         for core in range(2):
             columns = slice((2 * core + net) * HD, (2 * core + net + 1) * HD)
             key_values[:, columns] = total[net, :, core * HD : (core + 1) * HD].astype(BF16)
-    settle(len(sent))
 
 
 def hand_over(*refs):

time: 74.2 us -> 74.1 us (level)
  no operation moved by 1% of the time
where the time goes in v6:
time: 74.1 us; the launch traced here: 73.9 us
  Pallas kernels  73.3 us (99%)
    pallas_call x1, Pallas kernels, per_device(): pl.pallas_call(functools.partial(kernel, n, d_model), out_shape=outs, in_...  72.4 us

profile of v6, /device:TPU:1, one launch (start us, length us, event | category | flops | bytes accessed | tf_op | source)
XLA Modules:
  0.0 73.9 jit_solution(17132755301853769768)
XLA Ops:
  0.6 72.4 %shard_map.85 = (f32[2,64,512]{2,1,0:T(8,128)S(1)}, f32[2,64,512]{2,1,0:T(8,128)S(1)}, bf16[256,512]{1,0:T(8,128)(2,1)S(1)}) custom-call(s32[1,8]{1,0:T(1,128)} %table_in.1, f32[2,64,512]{2,1,0:T(8,128)} %master_in.1, f32[2,64,512]{2,1,0:T(8,128)} %momentum_in.1, f32[2,64,512]{2,1,0:T(8,128)} %gradient_in.1, bf16[256,2048]{1,0:T(8,128)(2,1)} %tokens_in.1, ...), custom_call_target="tpu_custom_call" | custom-call | tf_op jit(solution)/shard_map/pallas_call | solution.py:553
  73.0 0.9 %shard_map.86 = (f32[2,64,512]{2,1,0:T(8,128)}, f32[2,64,512]{2,1,0:T(8,128)}, bf16[256,512]{1,0:T(8,128)(2,1)}) custom-call(f32[2,64,512]{2,1,0:T(8,128)S(1)} %get-tuple-element.6.refs_0_, f32[2,64,512]{2,1,0:T(8,128)S(1)} %get-tuple-element.7.refs_1_, bf16[256,512]{1,0:T(8,128)(2,1)S(1)} %get-tuple-element.8.refs_2_), custom_call_target="tpu_custom_call" | custom-call | tf_op jit(solution)/shard_map/pallas_call | solution.py:566

commit v7 on v6

--- a/solution.py
+++ b/solution.py
@@ -474,11 +474,13 @@
     work = (
         (lambda: ring(1, 1), tokens_one, lambda: settle(marks[0]), lambda: marks.append(len(sent))),
         (lambda: ring(3, 0), tokens_three),
-        (lambda: ring(1, 2), tokens_two, lambda: normalise(tokens, 0), lambda: settle(marks[1])),
-        (lambda: ring(2, 1), lambda: marks.append(len(sent)), lambda: normalise(came_tokens.at[0], -1),
-         lambda: normalise(came_tokens.at[2], 1), lambda: normalise(came_tokens.at[1], 2)),
-        (lambda: ring(2, 2), own_block, functools.partial(distance, 1) if half > 1 else share),
-        (lambda: ring(3, 1), lambda: settle(marks[2]), lambda: ring(3, 2)),
+        (lambda: ring(1, 2), tokens_two, lambda: normalise(tokens, 0),
+         lambda: normalise(came_tokens.at[0], -1)),
+        (lambda: ring(2, 1), lambda: marks.append(len(sent)), lambda: normalise(came_tokens.at[2], 1),
+         lambda: normalise(came_tokens.at[1], 2)),
+        (lambda: ring(2, 2), own_block, lambda: settle(marks[1])),
+        (lambda: ring(3, 1), functools.partial(distance, 1) if half > 1 else share),
+        (lambda: ring(3, 2), lambda: settle(marks[2])),
     )
     for tasks in work:
         for task in tasks:

time: 74.1 us -> 74.1 us (level)
  no operation moved by 1% of the time
where the time goes in v7:
time: 74.1 us; the launch traced here: 73.9 us
  Pallas kernels  73.3 us (99%)
    pallas_call x1, Pallas kernels, per_device(): pl.pallas_call(functools.partial(kernel, n, d_model), out_shape=outs, in_...  72.4 us

profile of v7, /device:TPU:1, one launch (start us, length us, event | category | flops | bytes accessed | tf_op | source)
XLA Modules:
  0.0 73.9 jit_solution(14847517602435687122)
XLA Ops:
  0.6 72.4 %shard_map.85 = (f32[2,64,512]{2,1,0:T(8,128)S(1)}, f32[2,64,512]{2,1,0:T(8,128)S(1)}, bf16[256,512]{1,0:T(8,128)(2,1)S(1)}) custom-call(s32[1,8]{1,0:T(1,128)} %table_in.1, f32[2,64,512]{2,1,0:T(8,128)} %master_in.1, f32[2,64,512]{2,1,0:T(8,128)} %momentum_in.1, f32[2,64,512]{2,1,0:T(8,128)} %gradient_in.1, bf16[256,2048]{1,0:T(8,128)(2,1)} %tokens_in.1, ...), custom_call_target="tpu_custom_call" | custom-call | tf_op jit(solution)/shard_map/pallas_call | solution.py:555
  73.0 0.9 %shard_map.86 = (f32[2,64,512]{2,1,0:T(8,128)}, f32[2,64,512]{2,1,0:T(8,128)}, bf16[256,512]{1,0:T(8,128)(2,1)}) custom-call(f32[2,64,512]{2,1,0:T(8,128)S(1)} %get-tuple-element.6.refs_0_, f32[2,64,512]{2,1,0:T(8,128)S(1)} %get-tuple-element.7.refs_1_, bf16[256,512]{1,0:T(8,128)(2,1)S(1)} %get-tuple-element.8.refs_2_), custom_call_target="tpu_custom_call" | custom-call | tf_op jit(solution)/shard_map/pallas_call | solution.py:568

commit v8 on v6

--- a/solution.py
+++ b/solution.py
@@ -334,18 +334,30 @@
     def csem(net, offset, g):
         return core_send.at[net, offset % n, g], core_recv.at[net, offset % n, g]
 
-    fresh = []
+    fresh, came = [], {}
+    used = [g for g in range(3) if groups[g][0] < groups[g][1]]
+
+    def block_of(net, offset, core):
+        return weights.at[core, net, at(ring_axis[net], offset, n)]
 
     def share():
         while fresh:
             net, offset, g = fresh.pop(0)
-            moving = sub(net, offset, g)
-            send(moving, moving, csem(net, offset, g), partner)
+            if offset % n == half:
+                moving = sub(net, offset, g)
+                send(moving, moving, csem(net, offset, g), partner)
+                continue
+            came[net, offset] = came.get((net, offset), 0) + 1
+            if came[net, offset] == len(used):
+                moving = block_of(net, offset, c)
+                send(moving, moving, csem(net, offset, 0), partner)
 
     def shared(net, offset):
-        for g, (low, high) in enumerate(groups):
-            if low < high:
-                arrived(sub(net, offset, g, 1 - c), csem(net, offset, g), partner)
+        if offset % n != half:
+            arrived(block_of(net, offset, 1 - c), csem(net, offset, 0), partner)
+            return
+        for g in used:
+            arrived(sub(net, offset, g, 1 - c), csem(net, offset, g), partner)
 
     def goes(way, s, g):
         low, high = groups[g]

time: 74.1 us -> 74.3 us (level)
  no operation moved by 1% of the time
where the time goes in v8:
time: 74.3 us; the launch traced here: 74 us
  Pallas kernels  73.4 us (99%)
    pallas_call x1, Pallas kernels, per_device(): pl.pallas_call(functools.partial(kernel, n, d_model), out_shape=outs, in_...  72.5 us

profile of v8, /device:TPU:1, one launch (start us, length us, event | category | flops | bytes accessed | tf_op | source)
XLA Modules:
  0.0 74.0 jit_solution(9936130427581104215)
XLA Ops:
  0.6 72.5 %shard_map.85 = (f32[2,64,512]{2,1,0:T(8,128)S(1)}, f32[2,64,512]{2,1,0:T(8,128)S(1)}, bf16[256,512]{1,0:T(8,128)(2,1)S(1)}) custom-call(s32[1,8]{1,0:T(1,128)} %table_in.1, f32[2,64,512]{2,1,0:T(8,128)} %master_in.1, f32[2,64,512]{2,1,0:T(8,128)} %momentum_in.1, f32[2,64,512]{2,1,0:T(8,128)} %gradient_in.1, bf16[256,2048]{1,0:T(8,128)(2,1)} %tokens_in.1, ...), custom_call_target="tpu_custom_call" | custom-call | tf_op jit(solution)/shard_map/pallas_call | solution.py:565
  73.1 0.9 %shard_map.86 = (f32[2,64,512]{2,1,0:T(8,128)}, f32[2,64,512]{2,1,0:T(8,128)}, bf16[256,512]{1,0:T(8,128)(2,1)}) custom-call(f32[2,64,512]{2,1,0:T(8,128)S(1)} %get-tuple-element.6.refs_0_, f32[2,64,512]{2,1,0:T(8,128)S(1)} %get-tuple-element.7.refs_1_, bf16[256,512]{1,0:T(8,128)(2,1)S(1)} %get-tuple-element.8.refs_2_), custom_call_target="tpu_custom_call" | custom-call | tf_op jit(solution)/shard_map/pallas_call | solution.py:578
